TPU v7x, 256 devices: a whole 4x4x8 slice. The times are simulated.
256 devices in a mesh: ctx: 16 (over z, core), tp: 16 (over x, y).
Axes of the slice: x: 4, y: 4, z: 8, core: 2. Of those that a mesh axis runs over, the one named last changes fastest.
Arguments:
- tokens: bfloat16 [4096, 4096], P('ctx', 'tp'), may hold values from -6 to 6
- w_z: bfloat16 [4096, 8192], P(None, 'tp'), may hold values from -0.09375 to 0.09375
- w_x: bfloat16 [4096, 8192], P(None, 'tp'), may hold values from -0.09375 to 0.09375
- w_bc: bfloat16 [4096, 2048], P(None, 'tp'), may hold values from -0.09375 to 0.09375
- conv_x: float32 [4, 8192], P(None, 'tp'), may hold values from -3 to 3
- conv_bc: float32 [4, 2048], P(None, 'tp'), may hold values from -3 to 3
- bias_x: float32 [8192], P('tp'), may hold values from -0.5 to 0.5
- bias_bc: float32 [2048], P('tp'), may hold values from -0.5 to 0.5
- decay_logarithm: float32 [4096, 128], P('ctx', 'tp'), may hold values from -1.3 to 0, as said below
- head_step: float32 [128], P('tp'), may hold values from 0 to 0.3, as said below
- skip: float32 [128], P('tp'), may hold values from 0.5 to 1.5
- gain: float32 [8192], P('tp'), may hold values from 0.5 to 1.5
Outputs:
- normed: bfloat16 [4096, 8192], P('ctx', 'tp')
Inputs may be any that keep to these rules, and one draw needn't show every extreme that they name: decay_logarithm is negative. head_step is positive.
All inputs are finite; a program needn't handle non-finite values.
Results may differ from a plain program's by a relative error of at most 0.0095.
Values may be sent and summed in bfloat16 or wider, within the bound.
A program may use at most 64 MiB of HBM per device.

v0:
```python
import jax
import jax.numpy as jnp
from jax import lax
from jax.sharding import Mesh
from jax.sharding import PartitionSpec as P

KERNEL = 4
STRETCH = 256
CTX = ("ctx_0", "ctx_1")


def joined_along(tiles, dim):
    tiles = jnp.moveaxis(tiles, 0, dim)
    shape = tiles.shape
    return tiles.reshape(*shape[:dim], shape[dim] * shape[dim + 1], *shape[dim + 2 :])


def copy_for_each(shard, axis):
    size = lax.axis_size(axis)
    return lax.all_to_all(
        jnp.broadcast_to(shard[None], (size, *shard.shape)), axis, 0, 0, tiled=True
    )


def collect(shard, axis, dim):
    return joined_along(copy_for_each(shard, axis), dim)


def shifted(block, axis, distance):
    devices = range(lax.axis_size(axis))
    route = [(i - distance, i) for i in devices if i - distance in devices]
    return lax.ppermute(block, axis, route)


def partner(value, axis, distance):
    mask = 2**distance
    pairs = [(source, source ^ mask) for source in range(lax.axis_size(axis))]
    return lax.ppermute(value, axis, pairs)


def neutral_like(shard, identity):
    return jax.tree.map(
        lambda a, e: jnp.broadcast_to(jnp.asarray(e, a.dtype), a.shape), shard, identity
    )


def carried_in(shard, axes, combine, identity):
    before = start = neutral_like(shard, identity)
    running = shard
    for axis in reversed(axes):
        size, place = (lax.axis_size(axis), lax.axis_index(axis))
        pieces = jax.tree.map(lambda part: lax.all_gather(part, axis), running)
        inside, running = (start, start)
        for k in range(size):
            passed = k < place
            running = combine(running, jax.tree.map(lambda part: part[k], pieces))
            inside = jax.tree.map(lambda new, old: jnp.where(passed, new, old), running, inside)
        before = combine(inside, before)
    return before


def state_combine(earlier, later):
    return (earlier[0] + later[0], jnp.exp(later[0])[:, None, None] * earlier[1] + later[1])


def local(
    tokens, w_z, w_x, w_bc, conv_x, conv_bc, bias_x, bias_bc, decay_logarithm, head_step, skip, gain
):
    tok_rows = tokens.shape[0]
    x_width = w_x.shape[1]
    bc_width = w_bc.shape[1]
    heads_local = head_step.shape[0]
    head_dim = x_width // heads_local
    gathered = collect(tokens, "tp", 1)
    gate_sum = jnp.dot(gathered, w_z, preferred_element_type=jnp.float32)
    x_sum = jnp.dot(gathered, w_x, preferred_element_type=jnp.float32)
    bc_sum = jnp.dot(gathered, w_bc, preferred_element_type=jnp.float32)
    gate_in = gate_sum.astype(jnp.bfloat16)
    x_pre = x_sum.astype(jnp.bfloat16)
    bc_pre = bc_sum.astype(jnp.bfloat16)
    pre_conv = jnp.concatenate([x_pre, bc_pre], axis=1)
    rim_rows = shifted(pre_conv[tok_rows - (KERNEL - 1) :], CTX, 1)
    extended = jnp.concatenate([rim_rows, pre_conv], axis=0).astype(jnp.float32)
    conv_taps = jnp.concatenate([conv_x, conv_bc], axis=1)
    conv_bias = jnp.concatenate([bias_x, bias_bc], axis=0)
    conv_total = conv_bias[None, :] + jnp.zeros((tok_rows, x_width + bc_width), jnp.float32)
    for offset in range(KERNEL):
        conv_total = conv_total + conv_taps[offset][None, :] * extended[offset : offset + tok_rows]
    conv_out = jax.nn.silu(conv_total).astype(jnp.bfloat16)
    x_conv = conv_out[:, :x_width]
    own_bc = conv_out[:, x_width:]
    other_bc = partner(own_bc, "tp", 0)
    holds_b = lax.axis_index("tp") % 2 == 0
    b_proj = jnp.where(holds_b, own_bc, other_bc)
    c_proj = jnp.where(holds_b, other_bc, own_bc)
    stretch_len = STRETCH
    stretch_count = tok_rows // stretch_len
    x_float = x_conv.astype(jnp.float32).reshape(stretch_count, stretch_len, heads_local, head_dim)
    cum_decay = jnp.cumsum(decay_logarithm.reshape(stretch_count, stretch_len, heads_local), axis=1)
    b_stretches = b_proj.reshape(stretch_count, stretch_len, bc_width)
    c_stretches = c_proj.reshape(stretch_count, stretch_len, bc_width)
    scores = jnp.einsum(
        "cin,cjn->cij", c_stretches, b_stretches, preferred_element_type=jnp.float32
    )
    causal = jnp.tril(jnp.ones((stretch_len, stretch_len), dtype=bool))[None, :, :, None]
    pair_diff = cum_decay[:, :, None, :] - cum_decay[:, None, :, :]
    segment = jnp.where(causal, jnp.exp(jnp.where(causal, pair_diff, 0.0)), 0.0)
    mixing = segment * scores[:, :, :, None] * head_step
    intra_out = jnp.einsum("cijh,cjhp->cihp", mixing, x_float, precision=lax.Precision.HIGHEST)
    b_float = b_stretches.astype(jnp.float32)
    c_float = c_stretches.astype(jnp.float32)
    end_weight = jnp.exp(cum_decay[:, -1:, :] - cum_decay) * head_step
    stretch_states = jnp.einsum(
        "cjh,cjhp,cjn->chpn", end_weight, x_float, b_float, precision=lax.Precision.HIGHEST
    )
    stretch_decay = cum_decay[:, -1, :]

    def advance(state, item):
        added, decay_sum = item
        return (jnp.exp(decay_sum)[:, None, None] * state + added, state)

    zero_state = jnp.zeros((heads_local, head_dim, bc_width), jnp.float32)
    section_final_state, prior_section_state = lax.scan(
        advance, zero_state, (stretch_states, stretch_decay)
    )
    total_decay = jnp.sum(stretch_decay, axis=0)
    _, incoming = carried_in(
        (total_decay, section_final_state),
        CTX,
        state_combine,
        (jnp.zeros_like(total_decay), zero_state),
    )
    prefix_decay = jnp.cumsum(stretch_decay, axis=0) - stretch_decay
    entering = prior_section_state + jnp.exp(prefix_decay)[:, :, None, None] * incoming[None]
    inter_out = (
        jnp.einsum("cin,chpn->cihp", c_float, entering, precision=lax.Precision.HIGHEST)
        * jnp.exp(cum_decay)[:, :, :, None]
    )
    head_out = (intra_out + inter_out).reshape(tok_rows, heads_local, head_dim)
    head_out = head_out + skip[None, :, None] * x_conv.astype(jnp.float32).reshape(
        tok_rows, heads_local, head_dim
    )
    gated = head_out.reshape(tok_rows, x_width) * jax.nn.silu(gate_in.astype(jnp.float32))
    local_square = jnp.sum(gated * gated, axis=1)
    other_square = partner(local_square, "tp", 0)
    mean_square = (local_square + other_square) / (2 * x_width)
    scaled = gated * lax.rsqrt(mean_square + 1e-05)[:, None]
    return (scaled * gain[None, :]).astype(jnp.bfloat16)


def solution(mesh):
    split = Mesh(mesh.devices.reshape(8, 2, mesh.shape["tp"]), ("ctx_0", "ctx_1", "tp"))
    return jax.shard_map(
        local,
        mesh=split,
        in_specs=(
            P(CTX, "tp"),
            P(None, "tp"),
            P(None, "tp"),
            P(None, "tp"),
            P(None, "tp"),
            P(None, "tp"),
            P("tp"),
            P("tp"),
            P(CTX, "tp"),
            P("tp"),
            P("tp"),
            P("tp"),
        ),
        out_specs=P(CTX, "tp"),
        check_vma=False,
    )
```

profile of v0, /device:TPU:6, one launch (start us, length us, event | category | flops | bytes accessed | tf_op | source)
XLA Modules:
  0.0 130.1 jit_solution(3641135388911266646)
XLA Ops:
  6.5 1.1 copy.29
  7.6 1.5 %broadcast_in_dim.29 = bf16[16,256,256]{1,2,0:T(8,128)(2,1)} broadcast(bf16[256,256]{0,1:T(8,128)(2,1)S(1)} %copy.29), dimensions={1,2} | broadcast | bytes 2228224 | tf_op jit(solution)/shard_map/broadcast_in_dim | solution.py:21
  9.2 7.6 %all-to-all-start = ((bf16[16,256,256]{1,2,0:T(8,128)(2,1)}), bf16[16,256,256]{1,2,0:T(8,128)(2,1)S(1)}, u32[]{:S(2)}, u32[]{:S(2)}) async-start(bf16[16,256,256]{1,2,0:T(8,128)(2,1)} %broadcast_in_dim.29), calls=%async_computation | async-start | bytes 4194304 | tf_op jit(solution)/shard_map/all_to_all | solution.py:20
  18.5 1.8 %all-gather = f32[2,1,8]{2,1,0:T(1,128)S(1)} all-gather(f32[1,1,8]{2,1,0:T(1,128)S(1)} %copy.32), channel_id=2, replica_groups=mesh['ctx_0'=8,'ctx_1'=2,'tp'=16] {'ctx_1'}, dimensions={0}, use_global_device_ids=true | all-gather | bytes 96 | tf_op jit(solution)/shard_map/all_gather | solution.py:52
  21.0 23.4 %all-to-all-done = bf16[16,256,256]{1,2,0:T(8,128)(2,1)S(1)} async-done(((bf16[16,256,256]{1,2,0:T(8,128)(2,1)}), bf16[16,256,256]{1,2,0:T(8,128)(2,1)S(1)}, u32[]{:S(2)}, u32[]{:S(2)}) %all-to-all-start) | async-done | bytes 2097184 | tf_op jit(solution)/shard_map/all_to_all | solution.py:20
  44.4 0.8 convolution_convert_fusion.2
  45.2 3.5 %convolution_convert_fusion.1 = bf16[256,512]{1,0:T(8,128)(2,1)S(1)} fusion(bf16[256,4096]{0,1:T(8,128)(2,1)S(1)} %bitcast.97, bf16[4096,512]{1,0:T(8,128)(2,1)} %param.14), kind=kOutput, calls=%fused_computation.13 | convolution fusion | flops 1073872896 | bytes 6553600 | tf_op jit(solution)/shard_map/dot_general | solution.py:76
  48.7 1.3 collective-permute-start
  50.0 0.8 collective-permute-done
  53.8 1.8 %copy.31 = bf16[256,512]{0,1:T(8,128)(2,1)} copy(bf16[256,512]{1,0:T(8,128)(2,1)} %slice.157) | data formatting | bytes 524288 | tf_op jit(solution)/shard_map/slice | solution.py:90
  55.6 0.8 collective-permute-done.1
  56.4 1.4 %convolution_add_fusion = f32[8,64,128]{2,1,0:T(8,128)S(1)} fusion(bf16[256,8,64]{0,2,1:T(8,128)(2,1)} %bitcast.99, f32[256,8]{0,1:T(8,128)S(1)} %multiply_bitcast_fusion, f32[8]{0:T(128)} %get-tuple-element.41, bf16[256,128]{1,0:T(8,128)(2,1)S(1)} %collective-permute-done.1, pred[]{:T(512)S(6)} %eq.5, bf16[256,640]{1,0:T(8,128)(2,1)S(1)} %multiply_convert_fusion), kind=kOutput, calls=%fused_computation.14 | convolution fusion | flops 201687040 | bytes 663585 | tf_op jit(solution)/shard_map/cjh,cjhp,cjn->chpn/dot_general | solution.py:113
  57.8 3.3 %all-gather.1 = f32[16,64,128]{2,1,0:T(8,128)S(1)} all-gather(f32[8,64,128]{2,1,0:T(8,128)S(1)} %convolution_add_fusion), channel_id=3, replica_groups=mesh['ctx_0'=8,'ctx_1'=2,'tp'=16] {'ctx_1'}, dimensions={0}, use_global_device_ids=true | all-gather | bytes 786432 | tf_op jit(solution)/shard_map/all_gather | solution.py:52
  61.1 0.8 copy-done.1
  61.9 1.5 %fusion.31 = f32[1,8,64,128]{3,2,1,0:T(8,128)} fusion(f32[16,64,128]{2,1,0:T(8,128)S(1)} %all-gather.1, f32[8]{0:T(128)} %get-tuple-element.38, f32[8]{0:T(128)} %get-tuple-element.39), kind=kLoop, calls=%fused_computation.51 | loop fusion | flops 196608 | bytes 786496 | tf_op jit(solution)/shard_map/add | solution.py:63
  64.2 20.8 %all-gather.2 = f32[8,1,8]{2,1,0:T(1,128)S(1)} all-gather(f32[1,1,8]{2,1,0:T(1,128)} %get-tuple-element.25), channel_id=4, replica_groups=mesh['ctx_0'=8,'ctx_1'=2,'tp'=16] {'ctx_0'}, dimensions={0}, use_global_device_ids=true | all-gather | bytes 288 | tf_op jit(solution)/shard_map/all_gather | solution.py:52
  86.6 3.5 %fusion.7 = f32[1,256,8,64]{1,3,2,0:T(8,128)} fusion(bf16[256,8,64]{0,2,1:T(8,128)(2,1)} %bitcast.100, f32[8]{0:T(128)} %param.21, f32[256,256]{1,0:T(8,128)S(1)} %fusion.75, f32[256,8]{0,1:T(8,128)S(1)} %fusion.76, pred[256,256]{1,0:T(8,128)(4,1)S(1)} %iota_compare_fusion), kind=kOutput, calls=%fused_computation.7 | convolution fusion | flops 405274624 | bytes 1122336 | tf_op jit(solution)/shard_map/cijh,cjhp->cihp/dot_general | solution.py:109
  90.1 19.5 %all-gather.5.cloned.1.call-done = f32[8,8,64,128]{3,2,1,0:T(8,128)} async-done(((f32[1,8,64,128]{3,2,1,0:T(8,128)}), f32[8,8,64,128]{3,2,1,0:T(8,128)}) %all-gather.5.cloned.1.call-update) | async-done | bytes 2097168 | tf_op jit(solution)/shard_map/all_gather | solution.py:52
  109.7 3.3 %fusion.11 = f32[1,256,8,64]{1,3,2,0:T(8,128)} fusion(f32[1,256,8,64]{1,3,2,0:T(8,128)} %fusion.7, f32[8,8,64,128]{3,2,1,0:T(8,128)} %all-gather.5.cloned.1.call-done, f32[256,8]{0,1:T(8,128)S(1)} %copy-done.3, f32[1,8,64,128]{3,2,1,0:T(8,128)} %fusion.31, f32[16,64,128]{2,1,0:T(8,128)} %copy-done.1, f32[8]{0:T(128)S(1)} %copy-done.7, ...), kind=kOutput, calls=%fused_computation.10 | convolution fusion | flops 203522048 | bytes 3814923 | tf_op jit(solution)/shard_map/cin,chpn->cihp/dot_general | solution.py:136
  112.9 2.0 %copy.33 = f32[256,512]{1,0:T(8,128)} copy(f32[256,512]{0,1:T(8,128)} %bitcast.101) | data formatting | bytes 1048576 | tf_op jit(solution)/shard_map/reshape | solution.py:139
  115.0 3.8 %multiply_reduce_fusion = (f32[256]{0:T(256)S(1)}, f32[256,512]{1,0:T(8,128)S(1)}) fusion(bf16[256,4096]{0,1:T(8,128)(2,1)S(1)} %bitcast.98, bf16[4096,512]{1,0:T(8,128)(2,1)} %param.13, f32[256,512]{1,0:T(8,128)} %copy.33, bf16[256,640]{1,0:T(8,128)(2,1)S(1)} %multiply_convert_fusion, f32[512]{0:T(512)S(1)} %mul.307), kind=kOutput, calls=%fused_computation.32 | convolution fusion | flops 1075314432 | bytes 7605248 | tf_op jit(solution)/shard_map/dot_general | solution.py:75
  118.7 1.3 %collective-permute-start.2 = (f32[256]{0:T(256)S(1)}, f32[256]{0:T(256)S(1)}, u32[]{:S(2)}, u32[]{:S(2)}) collective-permute-start(f32[256]{0:T(256)S(1)} %get-tuple-element.42), channel_id=1, source_target_pairs={{0,1},{1,0},{2,3},{3,2},{4,5},{5,4},{6,7},{7,6},{8,9},{9,8},{10,11... | collective-permute-start | bytes 3080 | tf_op jit(solution)/shard_map/ppermute | solution.py:38
  120.0 2.3 %collective-permute-done.2 = f32[256]{0:T(256)S(1)} collective-permute-done((f32[256]{0:T(256)S(1)}, f32[256]{0:T(256)S(1)}, u32[]{:S(2)}, u32[]{:S(2)}) %collective-permute-start.2) | collective-permute-done | bytes 1056 | tf_op jit(solution)/shard_map/ppermute | solution.py:38
  122.4 0.8 multiply_convert_fusion.1
  (56 shorter events, 7.9 us)
Async XLA Ops:
  6.5 37.9 %copy-start = (bf16[4096,128]{1,0:T(8,128)(2,1)S(1)}, bf16[4096,128]{1,0:T(8,128)(2,1)}, u32[]{:S(2)}) copy-start(bf16[4096,128]{1,0:T(8,128)(2,1)} %param.15) | copy-start | bytes 3145732
  9.2 7.6 %copy-start.4 = (f32[256,8]{0,1:T(8,128)S(1)}, f32[256,8]{0,1:T(8,128)}, u32[]{:S(2)}) copy-start(f32[256,8]{0,1:T(8,128)} %param.20) | copy-start | bytes 24580
  9.2 11.1 %copy-start.5 = (f32[4,512]{1,0:T(4,128)S(1)}, f32[4,512]{1,0:T(4,128)}, u32[]{:S(2)}) copy-start(f32[4,512]{1,0:T(4,128)} %param.16) | copy-start | bytes 24580
  9.2 11.1 %copy-start.10 = (f32[4,128]{1,0:T(4,128)S(1)}, f32[4,128]{1,0:T(4,128)}, u32[]{:S(2)}) copy-start(f32[4,128]{1,0:T(4,128)} %param.17) | copy-start | bytes 6148
  9.2 11.8 %copy-start.12 = (f32[8]{0:T(128)S(1)}, f32[8]{0:T(128)}, u32[]{:S(2)}) copy-start(f32[8]{0:T(128)} %param.21) | copy-start | bytes 100
  9.2 35.2 %all-to-all-start = ((bf16[16,256,256]{1,2,0:T(8,128)(2,1)}), bf16[16,256,256]{1,2,0:T(8,128)(2,1)S(1)}, u32[]{:S(2)}, u32[]{:S(2)}) async-start(bf16[16,256,256]{1,2,0:T(8,128)(2,1)} %broadcast_in_dim.29), calls=%async_computation | async-start | bytes 4194304 | tf_op jit(solution)/shard_map/all_to_all | solution.py:20
  16.8 92.9 %all-gather.5.cloned.1.call-start = ((), (), s32[]{:S(2)}) async-start(), calls=%async_computation.1 | async-start | bytes 2359296 | tf_op jit(solution)/shard_map/all_gather | solution.py:52
  17.6 0.7 copy-start.2
  18.5 30.2 %copy-start.8 = (f32[8]{0:T(128)}, f32[8]{0:T(128)S(1)}, u32[]{:S(2)}) copy-start(f32[8]{0:T(128)S(1)} %get-tuple-element.29) | copy-start | bytes 100
  45.2 4.8 %copy-start.11 = (f32[512]{0:T(512)S(1)}, f32[512]{0:T(512)}, u32[]{:S(2)}) copy-start(f32[512]{0:T(512)} %param.18) | copy-start | bytes 6148
  45.2 4.8 %copy-start.13 = (f32[128]{0:T(128)S(1)}, f32[128]{0:T(128)}, u32[]{:S(2)}) copy-start(f32[128]{0:T(128)} %param.19) | copy-start | bytes 1540
  48.7 3.8 %copy-start.9 = (f32[8]{0:T(128)S(1)}, f32[8]{0:T(128)}, u32[]{:S(2)}) copy-start(f32[8]{0:T(128)} %copy-done.8) | copy-start | bytes 100
  48.7 2.1 %collective-permute-start = (bf16[3,640]{1,0:T(4,128)(2,1)S(1)}, bf16[3,640]{1,0:T(4,128)(2,1)S(1)}, u32[]{:S(2)}, u32[]{:S(2)}) collective-permute-start(bf16[3,640]{1,0:T(4,128)(2,1)S(1)} %pad_maximum_fusion), channel_id=1, source_target_pairs={{0,16},{16,32},{32,48},{48,64},{64,80},{80,96},{96,112},{112,128},... | collective-permute-start | bytes 11528 | tf_op jit(solution)/shard_map/ppermute | solution.py:32
  51.9 4.5 %collective-permute-start.1 = (bf16[256,128]{1,0:T(8,128)(2,1)}, bf16[256,128]{1,0:T(8,128)(2,1)S(1)}, u32[]{:S(2)}, u32[]{:S(2)}) collective-permute-start(bf16[256,128]{1,0:T(8,128)(2,1)} %slice.159), channel_id=1, source_target_pairs={{0,1},{1,0},{2,3},{3,2},{4,5},{5,4},{6,7},{7,6},{8,9},{9,8},{10,11... | collective-permute-start | bytes 196616 | tf_op jit(solution)/shard_map/ppermute | solution.py:38
  61.1 0.8 copy-start.1
  86.6 23.1 %copy-start.3 = (f32[256,8]{0,1:T(8,128)S(1)}, f32[256,8]{0,1:T(8,128)}, u32[]{:S(2)}) copy-start(f32[256,8]{0,1:T(8,128)} %get-tuple-element.26) | copy-start | bytes 24580
  86.6 23.0 %copy-start.7 = (f32[8]{0:T(128)S(1)}, f32[8]{0:T(128)}, u32[]{:S(2)}) copy-start(f32[8]{0:T(128)} %get-tuple-element.38) | copy-start | bytes 100
  114.9 7.4 %copy-start.6 = (f32[512]{0:T(512)S(1)}, f32[512]{0:T(512)}, u32[]{:S(2)}) copy-start(f32[512]{0:T(512)} %param.23) | copy-start | bytes 6148
  118.7 3.7 %collective-permute-start.2 = (f32[256]{0:T(256)S(1)}, f32[256]{0:T(256)S(1)}, u32[]{:S(2)}, u32[]{:S(2)}) collective-permute-start(f32[256]{0:T(256)S(1)} %get-tuple-element.42), channel_id=1, source_target_pairs={{0,1},{1,0},{2,3},{3,2},{4,5},{5,4},{6,7},{7,6},{8,9},{9,8},{10,11... | collective-permute-start | bytes 3080 | tf_op jit(solution)/shard_map/ppermute | solution.py:38
Sparse Core Ops, SparseCore 0:
  63.5 46.1 all-gather.4
where the time goes:
time: 130 us
  waiting for transfers between devices  46.8 us (36%)
  blocking collectives  25.9 us (20%)
  matrix products  16.3 us (13%)
  between operations  13.6 us (10%)
  starting transfers between devices  10.8 us (8%)
  local copies, waits for them, and re-layouts  9.9 us (8%)
  other arithmetic  6.77 us (5%)
    all_gather x3, blocking collectives, carried_in(): pieces = jax.tree.map(lambda part: lax.all_gather(part, axis), running)  25.9 us
    all_to_all x1, waiting for transfers between devices, copy_for_each(): lax.all_to_all(jnp.broadcast_to(shard[None], (size, *shard.shape)), axis,...  23.4 us
    all_gather x1, waiting for transfers between devices, carried_in(): pieces = jax.tree.map(lambda part: lax.all_gather(part, axis), running)  19.5 us
    all_to_all x1, starting transfers between devices, copy_for_each(): lax.all_to_all(jnp.broadcast_to(shard[None], (size, *shard.shape)), axis,...  7.57 us
    dot_general x1, matrix products, local(): gate_sum = jnp.dot(gathered, w_z, preferred_element_type=jnp.float32)  3.77 us
    dot_general x1, matrix products, local(): jnp.einsum('cijh,cjhp->cihp', mixing, x_float, precision=lax.Precision.HI...  3.53 us
    dot_general x1, matrix products, local(): x_sum = jnp.dot(gathered, w_x, preferred_element_type=jnp.float32)  3.46 us
    dot_general x1, matrix products, local(): jnp.einsum('cin,chpn->cihp', c_float, entering, precision=lax.Precision.H...  3.26 us
  transfers between devices with their start and end apart: 5, of which 5 were waited for; matrix products, arithmetic and copies ran while one was open for 9% of the time, Pallas kernels for 0%

commit v1 on v0

v1 whole, which is shorter than its diff:
```python
import jax
import jax.numpy as jnp
from jax import lax
from jax.experimental import pallas as pl
from jax.experimental.pallas import tpu as pltpu
from jax.sharding import PartitionSpec as P

MESH = pl.DeviceIdType.MESH
SIDE = 4
TAPS = 4
ROWS = 256
HALF = 128
FEAT = 256
SECTIONS = 16
LT = 4
F32 = jnp.float32
BF16 = jnp.bfloat16


def silu(v):
    return v / (1.0 + jnp.exp(-v))


def dot(a, b, **kw):
    return jnp.dot(a, b, preferred_element_type=F32, **kw)


def kernel(
    tok, wz, wx, wbc, conv_x, conv_bc, bias_x, bias_bc, decay_t, step, skip, gain, out,
    held, vz, vx, vbc, acc_z, acc_x, acc_bc, pre, rim_out, rim_in, xs, bc, seg, grow, end_w,
    tot_out, tot_in, st_out, st_in, en_out, en_in, y, sq_out, sq_in,
    w_sem, own_sem, g_send, g_recv, tot_send, tot_recv, rim_sem, bc_sem, st_sem, en_sem, sq_sem,
):
    ctx, tp = lax.axis_index("ctx"), lax.axis_index("tp")
    core = lax.rem(ctx, 2)
    x, y_at = lax.div(tp, SIDE), lax.rem(tp, SIDE)

    def at(px, py):
        return lax.rem(px + 2 * SIDE, SIDE) * SIDE + lax.rem(py + 2 * SIDE, SIDE)

    mate = at(x, y_at + 1 - 2 * lax.rem(y_at, 2))
    later = lax.rem(ctx + 1, SECTIONS)

    barrier = pltpu.get_barrier_semaphore()
    for px, py in ((1, 0), (-1, 0), (0, 1), (0, -1)):
        pl.semaphore_signal(
            barrier, inc=1, device_id=(ctx, at(x + px, y_at + py)), device_id_type=MESH
        )

    def greet(i, c):
        other = lax.rem(ctx + i, SECTIONS)
        pl.semaphore_signal(barrier, inc=1, device_id=(other, tp), device_id_type=MESH)
        return c

    lax.fori_loop(1, SECTIONS, greet, 0)

    weights = [
        pltpu.make_async_copy(a, b, w_sem.at[i])
        for i, (a, b) in enumerate(((wx, vx), (wbc, vbc), (wz, vz)))
    ]
    own = pltpu.make_async_copy(tok, held.at[tp], own_sem)
    own.start()
    for w in weights:
        w.start()
    pl.semaphore_wait(barrier, 4 + SECTIONS - 1)

    def slot(dx, dy):
        return at(x - dx, y_at - dy)

    def piece(s, half):
        return held.at[s, pl.ds(half * HALF, HALF), :]

    def dxy(half, first, second):
        return (second, first) if half == 0 else (first, second)

    def send(half, source, direction, along, landing):
        dx, dy = dxy(half, *source)
        px, py = dxy(half, *((direction, 0) if along == 0 else (0, direction)))
        first, second = landing
        s = slot(dx, dy)
        src = tok.at[pl.ds(half * HALF, HALF), :] if all(isinstance(v, int) and v == 0 for v in source) else piece(s, half)
        pltpu.make_async_remote_copy(
            src_ref=src,
            dst_ref=piece(s, half),
            send_sem=g_send,
            recv_sem=g_recv.at[half, first * SIDE + second],
            device_id=(ctx, at(x + px, y_at + py)),
            device_id_type=MESH,
        ).start()

    def arrived(half, first, second):
        p = piece(slot(*dxy(half, first, second)), half)
        pltpu.make_async_copy(p, p, g_recv.at[half, first * SIDE + second]).wait()

    def along_second(half, first):
        send(half, (first, 0), 1, 1, (first, 1))
        send(half, (first, 0), -1, 1, (first, 3))

    def across_second(half, first):
        flag = lax.rem(first + core, 2)
        send(half, (first, 1 + 2 * flag), 1 - 2 * flag, 1, (first, 2))

    def multiply(dx, dy, begin=False):
        s = slot(dx, dy)
        a = held[s]
        depth = pl.ds(pl.multiple_of(s * FEAT, FEAT), FEAT)
        for acc, v in ((acc_x, vx), (acc_bc, vbc), (acc_z, vz)):
            part = dot(a, v[depth, :])
            acc[...] = part if begin else acc[...] + part

    def multiply_all(count, offsets):
        def body(i, c):
            multiply(*offsets(i))
            return c

        lax.fori_loop(0, count, body, 0)

    for half in (0, 1):
        send(half, (0, 0), 1, 0, (1, 0))
        send(half, (0, 0), -1, 0, (3, 0))
    for half in (0, 1):
        along_second(half, 0)

    i0 = lax.broadcasted_iota(jnp.int32, (ROWS, ROWS), 0)
    i1 = lax.broadcasted_iota(jnp.int32, (ROWS, ROWS), 1)
    upper = (i0 <= i1).astype(F32)
    cum_t = dot(decay_t[...], upper, precision=lax.Precision.HIGHEST)
    lane = lax.broadcasted_iota(jnp.int32, (1, 128), 1)
    for t in range(LT):
        rows = jnp.concatenate(
            [jnp.broadcast_to(cum_t[2 * t + k : 2 * t + k + 1], (64, ROWS)) for k in (0, 1)], 0
        )
        cum = rows.T
        total = cum[ROWS - 1 : ROWS]
        step_row = jnp.where(lane < 64, step[2 * t], step[2 * t + 1])
        grow[t] = jnp.exp(cum)
        end_w[t] = jnp.exp(total - cum) * step_row
        tot_out[t] = jnp.broadcast_to(jnp.exp(total), (8, 128))

    my_tile = lax.div(ctx, 4)
    tot_in[ctx] = tot_out[my_tile]

    def send_total(i, c):
        o = lax.rem(ctx + i, SECTIONS)
        pltpu.make_async_remote_copy(
            src_ref=tot_out.at[lax.div(o, 4)],
            dst_ref=tot_in.at[ctx],
            send_sem=tot_send,
            recv_sem=tot_recv,
            device_id=(o, tp),
            device_id_type=MESH,
        ).start()
        return c

    lax.fori_loop(1, SECTIONS, send_total, 0)

    for half in (0, 1):
        arrived(half, 1, 0)
        arrived(half, 3, 0)
        send(half, (1 + 2 * core, 0), 1 - 2 * core, 0, (2, 0))
        along_second(half, 1)
        along_second(half, 3)
    for h in range(8):
        if h == 4:
            for half in (0, 1):
                arrived(half, 0, 1)
                arrived(half, 0, 3)
                across_second(half, 0)
        row = cum_t[h : h + 1]
        col = jnp.broadcast_to(row, (128, ROWS)).T
        col = jnp.concatenate([col, col], axis=1)
        keep = i0 >= i1
        seg[h] = jnp.where(keep, jnp.exp(jnp.where(keep, col - row, 0.0)), 0.0) * step[h]

    for half in (0, 1):
        arrived(half, 2, 0)
        along_second(half, 2)
    own.wait()
    for w in weights:
        w.wait()
    multiply(0, 0, True)

    def beside(i):
        o, swap = 1 + 2 * lax.rem(i, 2), lax.div(i, 2)
        return swap * o, (1 - swap) * o

    multiply_all(4, beside)
    for half in (0, 1):
        for first in (1, 3):
            arrived(half, first, 1)
            arrived(half, first, 3)
            across_second(half, first)
    multiply_all(4, lambda i: (1 + 2 * lax.rem(i, 2), 1 + 2 * lax.div(i, 2)))
    for half in (0, 1):
        arrived(half, 0, 2)
        arrived(half, 2, 1)
        arrived(half, 2, 3)
        across_second(half, 2)
    multiply_all(2, lambda i: (2 * (1 - i), 2 * i))
    for half in (0, 1):
        arrived(half, 1, 2)
        arrived(half, 3, 2)

    def far(i):
        o, swap = 1 + 2 * lax.rem(i, 2), lax.div(i, 2)
        return o + swap * (2 - o), 2 + swap * (o - 2)

    multiply_all(4, far)
    for half in (0, 1):
        arrived(half, 2, 2)
    multiply(2, 2)

    for t in range(LT + 1):
        p = acc_bc[...] if t == LT else acc_x[:, t * 128 : (t + 1) * 128]
        p = p.astype(BF16)
        rim_out[t] = p[ROWS - 16 :]
        pre[t, 8 : 8 + ROWS] = p.astype(F32)
    rim = pltpu.make_async_remote_copy(
        src_ref=rim_out,
        dst_ref=rim_in,
        send_sem=rim_sem.at[0],
        recv_sem=rim_sem.at[1],
        device_id=(later, tp),
        device_id_type=MESH,
    )
    rim.start()
    rim.wait_recv()

    def conv(t):
        pre[t, 0:8] = jnp.where(ctx > 0, rim_in[t].astype(F32)[8:], 0.0)
        cols = slice(0, 128) if t == LT else slice(t * 128, (t + 1) * 128)
        taps, bias = (conv_bc, bias_bc) if t == LT else (conv_x, bias_x)
        total = bias[:, cols] + jnp.zeros((ROWS, 128), F32)
        for k in range(TAPS):
            total = total + taps[k : k + 1, cols] * pre[t, 5 + k : 5 + k + ROWS]
        return silu(total).astype(BF16)

    side = lax.rem(tp, 2)
    bc[side] = conv(LT)
    swap = pltpu.make_async_remote_copy(
        src_ref=bc.at[side],
        dst_ref=bc.at[side],
        send_sem=bc_sem.at[0],
        recv_sem=bc_sem.at[1],
        device_id=(ctx, mate),
        device_id_type=MESH,
    )
    swap.start()
    for t in range(LT):
        xs[t] = conv(t)
    other = bc.at[1 - side]
    pltpu.make_async_copy(other, other, bc_sem.at[1]).wait()

    b_t = bc[0].astype(F32).T.astype(BF16)
    for t in range(LT):
        weighted = (xs[t].astype(F32) * end_w[t]).astype(BF16)
        st_out[4 * t : 4 * t + 4] = dot(b_t, weighted).reshape(4, 32, 128).astype(BF16)
    st_in[ctx] = st_out[ctx]

    def send_state(i, c):
        o = lax.rem(ctx + i, SECTIONS)
        pltpu.make_async_remote_copy(
            src_ref=st_out.at[o],
            dst_ref=st_in.at[ctx],
            send_sem=st_sem.at[0],
            recv_sem=st_sem.at[1],
            device_id=(o, tp),
            device_id_type=MESH,
        ).start()
        return c

    lax.fori_loop(1, SECTIONS, send_state, 0)

    scores = dot(bc[1], b_t)

    def intra(t):
        both = [dot((seg[2 * t + k] * scores).astype(BF16), xs[t]) for k in (0, 1)]
        skip_row = jnp.where(lane < 64, skip[2 * t], skip[2 * t + 1])
        y[t] = jnp.where(lane < 64, both[0], both[1]) + skip_row * xs[t].astype(F32)

    for t in range(2):
        intra(t)

    def all_but_one(ref, sem):
        part = ref.at[pl.ds(0, SECTIONS - 1)]
        pltpu.make_async_copy(part, part, sem).wait()

    all_but_one(tot_in, tot_recv)
    all_but_one(st_in, st_sem.at[1])
    state = jnp.zeros((32, 128), F32)
    for s in range(SECTIONS):
        en_out[s] = state.astype(BF16)
        state = tot_in[s][0:1] * state + st_in[s].astype(F32)
    en_in[ctx] = en_out[ctx]

    def send_entering(i, c):
        o = lax.rem(ctx + i, SECTIONS)
        pltpu.make_async_remote_copy(
            src_ref=en_out.at[o],
            dst_ref=en_in.at[ctx],
            send_sem=en_sem.at[0],
            recv_sem=en_sem.at[1],
            device_id=(o, tp),
            device_id_type=MESH,
        ).start()
        return c

    lax.fori_loop(1, SECTIONS, send_entering, 0)
    for t in range(2, LT):
        intra(t)
    for t in range(LT):
        g = acc_z[:, t * 128 : (t + 1) * 128].astype(BF16).astype(F32)
        acc_z[:, t * 128 : (t + 1) * 128] = silu(g)
    all_but_one(en_in, en_sem.at[1])

    squares = jnp.zeros((ROWS, 128), F32)
    for t in range(LT):
        entering = en_in[4 * t : 4 * t + 4].reshape(128, 128)
        gated = (y[t] + grow[t] * dot(bc[1], entering)) * acc_z[:, t * 128 : (t + 1) * 128]
        squares = squares + gated * gated
        y[t] = gated
    local = jnp.sum(squares.T, axis=0, keepdims=True)
    sq_out[...] = jnp.broadcast_to(local, (8, ROWS))
    norm = pltpu.make_async_remote_copy(
        src_ref=sq_out,
        dst_ref=sq_in,
        send_sem=sq_sem.at[0],
        recv_sem=sq_sem.at[1],
        device_id=(ctx, mate),
        device_id_type=MESH,
    )
    norm.start()
    norm.wait_recv()
    mean = (sq_out[0:1] + sq_in[0:1]) * (1.0 / (2 * LT * 128))
    scale = jnp.broadcast_to(lax.rsqrt(mean + 1e-5), (128, ROWS)).T
    for t in range(LT):
        cols = slice(t * 128, (t + 1) * 128)
        out[:, cols] = (y[t] * scale * gain[:, cols]).astype(BF16)

    norm.wait_send()
    rim.wait_send()
    swap.wait_send()
    all_but_one(held, g_send)
    all_but_one(tot_in, tot_send)
    all_but_one(st_out, st_sem.at[0])
    all_but_one(en_out, en_sem.at[0])


def local(tokens, w_z, w_x, w_bc, conv_x, conv_bc, bias_x, bias_bc, decay, step, skip, gain):
    hbm = pl.BlockSpec(memory_space=pl.ANY)
    vmem = pl.BlockSpec(memory_space=pltpu.VMEM)
    smem = pl.BlockSpec(memory_space=pltpu.SMEM)
    width = w_x.shape[1]
    dma = pltpu.SemaphoreType.DMA
    scratch = [
        pltpu.VMEM((16, ROWS, FEAT), BF16),
        pltpu.VMEM(w_z.shape, BF16),
        pltpu.VMEM(w_x.shape, BF16),
        pltpu.VMEM(w_bc.shape, BF16),
        pltpu.VMEM((ROWS, width), F32),
        pltpu.VMEM((ROWS, width), F32),
        pltpu.VMEM((ROWS, 128), F32),
        pltpu.VMEM((LT + 1, 8 + ROWS, 128), F32),
        pltpu.VMEM((LT + 1, 16, 128), BF16),
        pltpu.VMEM((LT + 1, 16, 128), BF16),
        pltpu.VMEM((LT, ROWS, 128), BF16),
        pltpu.VMEM((2, ROWS, 128), BF16),
        pltpu.VMEM((8, ROWS, ROWS), F32),
        pltpu.VMEM((LT, ROWS, 128), F32),
        pltpu.VMEM((LT, ROWS, 128), F32),
        pltpu.VMEM((LT, 8, 128), F32),
        pltpu.VMEM((SECTIONS, 8, 128), F32),
        pltpu.VMEM((SECTIONS, 32, 128), BF16),
        pltpu.VMEM((SECTIONS, 32, 128), BF16),
        pltpu.VMEM((SECTIONS, 32, 128), BF16),
        pltpu.VMEM((SECTIONS, 32, 128), BF16),
        pltpu.VMEM((LT, ROWS, 128), F32),
        pltpu.VMEM((8, ROWS), F32),
        pltpu.VMEM((8, ROWS), F32),
        dma((3,)),
        dma,
        dma,
        dma((2, 16)),
        dma,
        dma,
        dma((2,)),
        dma((2,)),
        dma((2,)),
        dma((2,)),
        dma((2,)),
    ]
    return pl.pallas_call(
        kernel,
        out_shape=jax.ShapeDtypeStruct((ROWS, width), BF16),
        in_specs=[hbm] * 4 + [vmem] * 5 + [smem] * 2 + [vmem],
        out_specs=vmem,
        scratch_shapes=scratch,
        compiler_params=pltpu.CompilerParams(
            collective_id=0, has_side_effects=True, vmem_limit_bytes=56 * 2**20
        ),
    )(
        tokens, w_z, w_x, w_bc, conv_x, conv_bc, bias_x.reshape(1, -1), bias_bc.reshape(1, -1),
        decay.T, step, skip, gain.reshape(1, -1),
    )


def solution(mesh):
    return jax.shard_map(
        local,
        mesh=mesh,
        in_specs=(
            P("ctx", "tp"),
            P(None, "tp"),
            P(None, "tp"),
            P(None, "tp"),
            P(None, "tp"),
            P(None, "tp"),
            P("tp"),
            P("tp"),
            P("ctx", "tp"),
            P("tp"),
            P("tp"),
            P("tp"),
        ),
        out_specs=P("ctx", "tp"),
        check_vma=False,
    )
```

time: 130 us -> 52.9 us (0.41)
  the two profiles are of different devices: /device:TPU:6 before, /device:TPU:1 now
where the time goes in v1:
time: 52.9 us; the launch traced here: 52.7 us
  Pallas kernels  51 us (96%)
  local copies, waits for them, and re-layouts  1.67 us (3%)
    pallas_call x1, Pallas kernels, local(): pl.pallas_call(kernel, out_shape=jax.ShapeDtypeStruct((ROWS, width), BF16...  51 us
    unnamed x1, local copies, waits for them, and re-layouts  1.67 us

profile of v1, /device:TPU:1, one launch (start us, length us, event | category | flops | bytes accessed | tf_op | source)
XLA Modules:
  0.0 52.7 jit_solution(6517606287505806691)
XLA Ops:
  0.0 51.0 %shard_map.118 = bf16[256,512]{1,0:T(8,128)(2,1)} custom-call(bf16[256,256]{1,0:T(8,128)(2,1)} %tok.1, bf16[4096,512]{1,0:T(8,128)(2,1)} %wz.1, bf16[4096,512]{1,0:T(8,128)(2,1)} %wx.1, bf16[4096,128]{1,0:T(8,128)(2,1)} %wbc.1, f32[4,512]{1,0:T(4,128)} %conv_x.1, f32[4,128]{1,0:T(4,128)} %conv_bc.1, f32[1,512]{1,0:T(1,128)} %bitcast.5, f32[1,128]{1,0:T(1,128)} %bitcast.7, ...), custom_call_target="tpu_custom_call" | custom-call | tf_op jit(solution)/shard_map/pallas_call | solution.py:392
  51.0 1.7 %copy.14 = bf16[256,512]{1,0:T(8,128)(2,1)} copy(bf16[256,512]{1,0:T(8,128)(2,1)} %shard_map.118) | data formatting | bytes 524288

commit v2 on v1

--- a/solution.py
+++ b/solution.py
@@ -12,6 +12,8 @@
 HALF = 128
 FEAT = 256
 SECTIONS = 16
+PEERS = 8
+SLICE = 64
 LT = 4
 F32 = jnp.float32
 BF16 = jnp.bfloat16
@@ -28,8 +30,9 @@
 def kernel(
     tok, wz, wx, wbc, conv_x, conv_bc, bias_x, bias_bc, decay_t, step, skip, gain, out,
     held, vz, vx, vbc, acc_z, acc_x, acc_bc, pre, rim_out, rim_in, xs, bc, seg, grow, end_w,
-    tot_out, tot_in, st_out, st_in, en_out, en_in, y, sq_out, sq_in,
-    w_sem, own_sem, g_send, g_recv, tot_send, tot_recv, rim_sem, bc_sem, st_sem, en_sem, sq_sem,
+    tot_out, tot_in, st_out, st_in, en_out, en_in, half_out, half_in, y, sq_out, sq_in,
+    w_sem, own_sem, g_send, g_recv, tot_send, tot_recv, rim_sem, bc_sem, st_send, st_recv,
+    en_send, en_recv, half_sem, sq_sem, up, down, facing,
 ):
     ctx, tp = lax.axis_index("ctx"), lax.axis_index("tp")
     core = lax.rem(ctx, 2)
@@ -39,20 +42,34 @@
         return lax.rem(px + 2 * SIDE, SIDE) * SIDE + lax.rem(py + 2 * SIDE, SIDE)
 
     mate = at(x, y_at + 1 - 2 * lax.rem(y_at, 2))
-    later = lax.rem(ctx + 1, SECTIONS)
+    z = lax.div(ctx, 2)
+    group, me = lax.div(ctx, PEERS), lax.rem(ctx, PEERS)
+    place = lax.rem(z, 4)
+    mirror = (7 - z) * 2 + core
+
+    def owner(o):
+        p = lax.div(o, 2)
+        return (p + group * (3 - 2 * p)) * 2 + lax.rem(o, 2)
+
+    mine = owner(me)
+
+    def signal(sem, section, column=None):
+        pl.semaphore_signal(
+            sem, inc=1, device_id=(section, tp if column is None else column), device_id_type=MESH
+        )
 
     barrier = pltpu.get_barrier_semaphore()
     for px, py in ((1, 0), (-1, 0), (0, 1), (0, -1)):
-        pl.semaphore_signal(
-            barrier, inc=1, device_id=(ctx, at(x + px, y_at + py)), device_id_type=MESH
-        )
-
-    def greet(i, c):
-        other = lax.rem(ctx + i, SECTIONS)
-        pl.semaphore_signal(barrier, inc=1, device_id=(other, tp), device_id_type=MESH)
-        return c
-
-    lax.fori_loop(1, SECTIONS, greet, 0)
+        signal(barrier, ctx, at(x + px, y_at + py))
+    signal(barrier, ctx + 1 - 2 * core)
+
+    @pl.when(z < 7)
+    def _():
+        signal(barrier, ctx + 2)
+
+    @pl.when(group == 0)
+    def _():
+        signal(barrier, mirror)
 
     weights = [
         pltpu.make_async_copy(a, b, w_sem.at[i])
@@ -62,7 +79,7 @@
     own.start()
     for w in weights:
         w.start()
-    pl.semaphore_wait(barrier, 4 + SECTIONS - 1)
+    pl.semaphore_wait(barrier, 5 + lax.min(z, 1) + group)
 
     def slot(dx, dy):
         return at(x - dx, y_at - dy)
@@ -121,6 +138,32 @@
     for half in (0, 1):
         along_second(half, 0)
 
+    @pl.when(group == 1)
+    def _():
+        signal(facing, mirror)
+
+    @pl.when(place == 3)
+    def _():
+        signal(up, ctx - 2)
+
+    def sweep_up(at_place):
+        @pl.when(place == at_place)
+        def _():
+            pl.semaphore_wait(up, 1)
+            if at_place == 0:
+                signal(down, ctx + 2)
+
+        @pl.when(jnp.logical_and(place == at_place, z > 0))
+        def _():
+            signal(up, ctx - 2)
+
+    def sweep_down(at_place):
+        @pl.when(place == at_place)
+        def _():
+            pl.semaphore_wait(down, 1)
+            if at_place < 3:
+                signal(down, ctx + 2)
+
     i0 = lax.broadcasted_iota(jnp.int32, (ROWS, ROWS), 0)
     i1 = lax.broadcasted_iota(jnp.int32, (ROWS, ROWS), 1)
     upper = (i0 <= i1).astype(F32)
@@ -136,23 +179,6 @@
         grow[t] = jnp.exp(cum)
         end_w[t] = jnp.exp(total - cum) * step_row
         tot_out[t] = jnp.broadcast_to(jnp.exp(total), (8, 128))
-
-    my_tile = lax.div(ctx, 4)
-    tot_in[ctx] = tot_out[my_tile]
-
-    def send_total(i, c):
-        o = lax.rem(ctx + i, SECTIONS)
-        pltpu.make_async_remote_copy(
-            src_ref=tot_out.at[lax.div(o, 4)],
-            dst_ref=tot_in.at[ctx],
-            send_sem=tot_send,
-            recv_sem=tot_recv,
-            device_id=(o, tp),
-            device_id_type=MESH,
-        ).start()
-        return c
-
-    lax.fori_loop(1, SECTIONS, send_total, 0)
 
     for half in (0, 1):
         arrived(half, 1, 0)
@@ -172,13 +198,13 @@
         keep = i0 >= i1
         seg[h] = jnp.where(keep, jnp.exp(jnp.where(keep, col - row, 0.0)), 0.0) * step[h]
 
-    for half in (0, 1):
-        arrived(half, 2, 0)
-        along_second(half, 2)
     own.wait()
     for w in weights:
         w.wait()
     multiply(0, 0, True)
+    for half in (0, 1):
+        arrived(half, 2, 0)
+        along_second(half, 2)
 
     def beside(i):
         o, swap = 1 + 2 * lax.rem(i, 2), lax.div(i, 2)
@@ -186,17 +212,25 @@
 
     multiply_all(4, beside)
     for half in (0, 1):
-        for first in (1, 3):
-            arrived(half, first, 1)
-            arrived(half, first, 3)
-            across_second(half, first)
+        arrived(half, 1, 1)
+        arrived(half, 1, 3)
+        across_second(half, 1)
+    sweep_up(2)
+    for half in (0, 1):
+        arrived(half, 3, 1)
+        arrived(half, 3, 3)
+        across_second(half, 3)
+    sweep_up(1)
     multiply_all(4, lambda i: (1 + 2 * lax.rem(i, 2), 1 + 2 * lax.div(i, 2)))
     for half in (0, 1):
         arrived(half, 0, 2)
+    sweep_up(0)
+    multiply_all(2, lambda i: (2 * (1 - i), 2 * i))
+    for half in (0, 1):
         arrived(half, 2, 1)
         arrived(half, 2, 3)
         across_second(half, 2)
-    multiply_all(2, lambda i: (2 * (1 - i), 2 * i))
+    sweep_down(1)
     for half in (0, 1):
         arrived(half, 1, 2)
         arrived(half, 3, 2)
@@ -206,9 +240,11 @@
         return o + swap * (2 - o), 2 + swap * (o - 2)
 
     multiply_all(4, far)
+    sweep_down(2)
     for half in (0, 1):
         arrived(half, 2, 2)
     multiply(2, 2)
+    sweep_down(3)
 
     for t in range(LT + 1):
         p = acc_bc[...] if t == LT else acc_x[:, t * 128 : (t + 1) * 128]
@@ -220,14 +256,44 @@
         dst_ref=rim_in,
         send_sem=rim_sem.at[0],
         recv_sem=rim_sem.at[1],
-        device_id=(later, tp),
+        device_id=(lax.min(ctx + 1, SECTIONS - 1), tp),
         device_id_type=MESH,
     )
-    rim.start()
-    rim.wait_recv()
+
+    @pl.when(z == 3)
+    def _():
+        pl.semaphore_wait(up, 1)
+
+    @pl.when(ctx < SECTIONS - 1)
+    def _():
+        rim.start()
+
+    tot_in[me] = tot_out[lax.div(mine, 2)]
+
+    def send_total(i, c):
+        q = lax.rem(me + i, PEERS)
+        pltpu.make_async_remote_copy(
+            src_ref=tot_out.at[lax.div(owner(q), 2)],
+            dst_ref=tot_in.at[me],
+            send_sem=tot_send,
+            recv_sem=tot_recv,
+            device_id=(group * PEERS + q, tp),
+            device_id_type=MESH,
+        ).start()
+        return c
+
+    lax.fori_loop(1, PEERS, send_total, 0)
+
+    @pl.when(ctx == 0)
+    def _():
+        rim_in[...] = jnp.zeros_like(rim_in)
+
+    @pl.when(ctx > 0)
+    def _():
+        rim.wait_recv()
 
     def conv(t):
-        pre[t, 0:8] = jnp.where(ctx > 0, rim_in[t].astype(F32)[8:], 0.0)
+        pre[t, 0:8] = rim_in[t].astype(F32)[8:]
         cols = slice(0, 128) if t == LT else slice(t * 128, (t + 1) * 128)
         taps, bias = (conv_bc, bias_bc) if t == LT else (conv_x, bias_x)
         total = bias[:, cols] + jnp.zeros((ROWS, 128), F32)
@@ -254,22 +320,22 @@
     b_t = bc[0].astype(F32).T.astype(BF16)
     for t in range(LT):
         weighted = (xs[t].astype(F32) * end_w[t]).astype(BF16)
-        st_out[4 * t : 4 * t + 4] = dot(b_t, weighted).reshape(4, 32, 128).astype(BF16)
-    st_in[ctx] = st_out[ctx]
+        st_out[2 * t : 2 * t + 2] = dot(b_t, weighted).reshape(2, SLICE, 128).astype(BF16)
+    st_in[me] = st_out[mine]
 
     def send_state(i, c):
-        o = lax.rem(ctx + i, SECTIONS)
+        q = lax.rem(me + i, PEERS)
         pltpu.make_async_remote_copy(
-            src_ref=st_out.at[o],
-            dst_ref=st_in.at[ctx],
-            send_sem=st_sem.at[0],
-            recv_sem=st_sem.at[1],
-            device_id=(o, tp),
+            src_ref=st_out.at[owner(q)],
+            dst_ref=st_in.at[me],
+            send_sem=st_send,
+            recv_sem=st_recv.at[me],
+            device_id=(group * PEERS + q, tp),
             device_id_type=MESH,
         ).start()
         return c
 
-    lax.fori_loop(1, SECTIONS, send_state, 0)
+    lax.fori_loop(1, PEERS, send_state, 0)
 
     scores = dot(bc[1], b_t)
 
@@ -278,44 +344,80 @@
         skip_row = jnp.where(lane < 64, skip[2 * t], skip[2 * t + 1])
         y[t] = jnp.where(lane < 64, both[0], both[1]) + skip_row * xs[t].astype(F32)
 
-    for t in range(2):
-        intra(t)
-
-    def all_but_one(ref, sem):
-        part = ref.at[pl.ds(0, SECTIONS - 1)]
-        pltpu.make_async_copy(part, part, sem).wait()
-
-    all_but_one(tot_in, tot_recv)
-    all_but_one(st_in, st_sem.at[1])
-    state = jnp.zeros((32, 128), F32)
-    for s in range(SECTIONS):
-        en_out[s] = state.astype(BF16)
-        state = tot_in[s][0:1] * state + st_in[s].astype(F32)
-    en_in[ctx] = en_out[ctx]
-
-    def send_entering(i, c):
-        o = lax.rem(ctx + i, SECTIONS)
-        pltpu.make_async_remote_copy(
-            src_ref=en_out.at[o],
-            dst_ref=en_in.at[ctx],
-            send_sem=en_sem.at[0],
-            recv_sem=en_sem.at[1],
-            device_id=(o, tp),
-            device_id_type=MESH,
-        ).start()
-        return c
-
-    lax.fori_loop(1, SECTIONS, send_entering, 0)
-    for t in range(2, LT):
+    for t in range(LT):
         intra(t)
     for t in range(LT):
         g = acc_z[:, t * 128 : (t + 1) * 128].astype(BF16).astype(F32)
         acc_z[:, t * 128 : (t + 1) * 128] = silu(g)
-    all_but_one(en_in, en_sem.at[1])
+
+    def all_but_one(ref, sem):
+        part = ref.at[pl.ds(0, ref.shape[0] - 1)]
+        pltpu.make_async_copy(part, part, sem).wait()
+
+    all_but_one(tot_in, tot_recv)
+    total_of_half = pltpu.make_async_remote_copy(
+        src_ref=half_out,
+        dst_ref=half_in,
+        send_sem=half_sem.at[0],
+        recv_sem=half_sem.at[1],
+        device_id=(lax.max(mirror, PEERS), tp),
+        device_id_type=MESH,
+    )
+
+    @pl.when(group == 0)
+    def _():
+        half_in[...] = jnp.zeros_like(half_in)
+
+    @pl.when(group == 1)
+    def _():
+        total_of_half.wait_recv()
+
+    def entering_copy(q):
+        return pltpu.make_async_remote_copy(
+            src_ref=en_out.at[q],
+            dst_ref=en_in.at[mine],
+            send_sem=en_send.at[q],
+            recv_sem=en_recv,
+            device_id=(group * PEERS + q, tp),
+            device_id_type=MESH,
+        )
+
+    def sends(q):
+        return jnp.logical_and(me != q, group * PEERS + q > 0)
+
+    state = half_in[...].astype(F32)
+    for q in range(PEERS):
+        en_out[q] = state.astype(BF16)
+
+        @pl.when(sends(q))
+        def _(q=q):
+            entering_copy(q).start()
+
+        @pl.when(me != q)
+        def _(q=q):
+            pltpu.make_async_copy(st_in.at[q], st_in.at[q], st_recv.at[q]).wait()
+
+        state = tot_in[q][0:1] * state + st_in[q].astype(F32)
+    half_out[...] = state.astype(BF16)
+
+    @pl.when(group == 0)
+    def _():
+        pl.semaphore_wait(facing, 1)
+        total_of_half.start()
+
+    en_in[mine] = en_out[me]
+
+    @pl.when(ctx == 0)
+    def _():
+        en_in[...] = jnp.zeros_like(en_in)
+
+    @pl.when(ctx > 0)
+    def _():
+        all_but_one(en_in, en_recv)
 
     squares = jnp.zeros((ROWS, 128), F32)
     for t in range(LT):
-        entering = en_in[4 * t : 4 * t + 4].reshape(128, 128)
+        entering = en_in[2 * t : 2 * t + 2].reshape(128, 128)
         gated = (y[t] + grow[t] * dot(bc[1], entering)) * acc_z[:, t * 128 : (t + 1) * 128]
         squares = squares + gated * gated
         y[t] = gated
@@ -338,12 +440,24 @@
         out[:, cols] = (y[t] * scale * gain[:, cols]).astype(BF16)
 
     norm.wait_send()
-    rim.wait_send()
     swap.wait_send()
     all_but_one(held, g_send)
     all_but_one(tot_in, tot_send)
-    all_but_one(st_out, st_sem.at[0])
-    all_but_one(en_out, en_sem.at[0])
+    all_but_one(st_out, st_send)
+
+    @pl.when(ctx < SECTIONS - 1)
+    def _():
+        rim.wait_send()
+
+    @pl.when(group == 0)
+    def _():
+        total_of_half.wait_send()
+
+    for q in range(PEERS):
+
+        @pl.when(sends(q))
+        def _(q=q):
+            entering_copy(q).wait_send()
 
 
 def local(tokens, w_z, w_x, w_bc, conv_x, conv_bc, bias_x, bias_bc, decay, step, skip, gain):
@@ -369,11 +483,13 @@
         pltpu.VMEM((LT, ROWS, 128), F32),
         pltpu.VMEM((LT, ROWS, 128), F32),
         pltpu.VMEM((LT, 8, 128), F32),
-        pltpu.VMEM((SECTIONS, 8, 128), F32),
-        pltpu.VMEM((SECTIONS, 32, 128), BF16),
-        pltpu.VMEM((SECTIONS, 32, 128), BF16),
-        pltpu.VMEM((SECTIONS, 32, 128), BF16),
-        pltpu.VMEM((SECTIONS, 32, 128), BF16),
+        pltpu.VMEM((PEERS, 8, 128), F32),
+        pltpu.VMEM((PEERS, SLICE, 128), BF16),
+        pltpu.VMEM((PEERS, SLICE, 128), BF16),
+        pltpu.VMEM((PEERS, SLICE, 128), BF16),
+        pltpu.VMEM((PEERS, SLICE, 128), BF16),
+        pltpu.VMEM((SLICE, 128), BF16),
+        pltpu.VMEM((SLICE, 128), BF16),
         pltpu.VMEM((LT, ROWS, 128), F32),
         pltpu.VMEM((8, ROWS), F32),
         pltpu.VMEM((8, ROWS), F32),
@@ -385,9 +501,15 @@
         dma,
         dma((2,)),
         dma((2,)),
+        dma,
+        dma((PEERS,)),
+        dma((PEERS,)),
+        dma,
         dma((2,)),
         dma((2,)),
-        dma((2,)),
+        pltpu.SemaphoreType.REGULAR,
+        pltpu.SemaphoreType.REGULAR,
+        pltpu.SemaphoreType.REGULAR,
     ]
     return pl.pallas_call(
         kernel,

time: 52.9 us -> 46.6 us (0.88)
  the two profiles are of different devices: /device:TPU:1 before, /device:TPU:224 now
where the time goes in v2:
time: 46.6 us; the launch traced here: 46.4 us
  Pallas kernels  44.7 us (96%)
  local copies, waits for them, and re-layouts  1.67 us (4%)
    pallas_call x1, Pallas kernels, local(): pl.pallas_call(kernel, out_shape=jax.ShapeDtypeStruct((ROWS, width), BF16...  44.7 us
    unnamed x1, local copies, waits for them, and re-layouts  1.67 us

profile of v2, /device:TPU:224, one launch (start us, length us, event | category | flops | bytes accessed | tf_op | source)
XLA Modules:
  0.0 46.4 jit_solution(10416147269085461365)
XLA Ops:
  0.0 44.7 %shard_map.118 = bf16[256,512]{1,0:T(8,128)(2,1)} custom-call(bf16[256,256]{1,0:T(8,128)(2,1)} %tok.1, bf16[4096,512]{1,0:T(8,128)(2,1)} %wz.1, bf16[4096,512]{1,0:T(8,128)(2,1)} %wx.1, bf16[4096,128]{1,0:T(8,128)(2,1)} %wbc.1, f32[4,512]{1,0:T(4,128)} %conv_x.1, f32[4,128]{1,0:T(4,128)} %conv_bc.1, f32[1,512]{1,0:T(1,128)} %bitcast.5, f32[1,128]{1,0:T(1,128)} %bitcast.7, ...), custom_call_target="tpu_custom_call" | custom-call | tf_op jit(solution)/shard_map/pallas_call | solution.py:514
  44.7 1.7 %copy.14 = bf16[256,512]{1,0:T(8,128)(2,1)} copy(bf16[256,512]{1,0:T(8,128)(2,1)} %shard_map.118) | data formatting | bytes 524288

commit v3 on v2

--- a/solution.py
+++ b/solution.py
@@ -45,11 +45,12 @@
     z = lax.div(ctx, 2)
     group, me = lax.div(ctx, PEERS), lax.rem(ctx, PEERS)
     place = lax.rem(z, 4)
-    mirror = (7 - z) * 2 + core
+    far_place = lax.rem(place + 2, 4)
+    facing_at = ((1 - group) * 4 + far_place) * 2 + core
 
     def owner(o):
-        p = lax.div(o, 2)
-        return (p + group * (3 - 2 * p)) * 2 + lax.rem(o, 2)
+        p = lax.rem(lax.div(o, 2) + 2 * group, 4)
+        return p * 2 + lax.rem(o, 2)
 
     mine = owner(me)
 
@@ -59,7 +60,7 @@
         )
 
     barrier = pltpu.get_barrier_semaphore()
-    for px, py in ((1, 0), (-1, 0), (0, 1), (0, -1)):
+    for px, py in ((1, 0), (-1, 0), (0, 1), (0, -1), (2, 0), (0, 2)):
         signal(barrier, ctx, at(x + px, y_at + py))
     signal(barrier, ctx + 1 - 2 * core)
 
@@ -69,7 +70,7 @@
 
     @pl.when(group == 0)
     def _():
-        signal(barrier, mirror)
+        signal(barrier, facing_at)
 
     weights = [
         pltpu.make_async_copy(a, b, w_sem.at[i])
@@ -79,7 +80,7 @@
     own.start()
     for w in weights:
         w.start()
-    pl.semaphore_wait(barrier, 5 + lax.min(z, 1) + group)
+    pl.semaphore_wait(barrier, 7 + lax.min(z, 1) + group)
 
     def slot(dx, dy):
         return at(x - dx, y_at - dy)
@@ -110,12 +111,21 @@
         pltpu.make_async_copy(p, p, g_recv.at[half, first * SIDE + second]).wait()
 
     def along_second(half, first):
+        if first == 3:
+
+            @pl.when(core == 0)
+            def _():
+                send(half, (first, 0), 2, 1, (first, 2))
+
         send(half, (first, 0), 1, 1, (first, 1))
         send(half, (first, 0), -1, 1, (first, 3))
 
     def across_second(half, first):
         flag = lax.rem(first + core, 2)
-        send(half, (first, 1 + 2 * flag), 1 - 2 * flag, 1, (first, 2))
+
+        @pl.when(jnp.logical_or(core == 1, first < 3))
+        def _():
+            send(half, (first, 1 + 2 * flag), 1 - 2 * flag, 1, (first, 2))
 
     def multiply(dx, dy, begin=False):
         s = slot(dx, dy)
@@ -133,6 +143,8 @@
         lax.fori_loop(0, count, body, 0)
 
     for half in (0, 1):
+        send(half, (0, 0), 2, 0, (2, 0))
+    for half in (0, 1):
         send(half, (0, 0), 1, 0, (1, 0))
         send(half, (0, 0), -1, 0, (3, 0))
     for half in (0, 1):
@@ -140,7 +152,7 @@
 
     @pl.when(group == 1)
     def _():
-        signal(facing, mirror)
+        signal(facing, facing_at)
 
     @pl.when(place == 3)
     def _():
@@ -181,10 +193,12 @@
         tot_out[t] = jnp.broadcast_to(jnp.exp(total), (8, 128))
 
     for half in (0, 1):
+        arrived(half, 2, 0)
+        along_second(half, 2)
+    for half in (0, 1):
         arrived(half, 1, 0)
+        along_second(half, 1)
         arrived(half, 3, 0)
-        send(half, (1 + 2 * core, 0), 1 - 2 * core, 0, (2, 0))
-        along_second(half, 1)
         along_second(half, 3)
     for h in range(8):
         if h == 4:
@@ -198,38 +212,35 @@
         keep = i0 >= i1
         seg[h] = jnp.where(keep, jnp.exp(jnp.where(keep, col - row, 0.0)), 0.0) * step[h]
 
+    for half in (0, 1):
+        arrived(half, 2, 1)
+        arrived(half, 2, 3)
+        across_second(half, 2)
     own.wait()
     for w in weights:
         w.wait()
     multiply(0, 0, True)
-    for half in (0, 1):
-        arrived(half, 2, 0)
-        along_second(half, 2)
 
     def beside(i):
         o, swap = 1 + 2 * lax.rem(i, 2), lax.div(i, 2)
         return swap * o, (1 - swap) * o
 
     multiply_all(4, beside)
+    sweep_up(2)
     for half in (0, 1):
         arrived(half, 1, 1)
         arrived(half, 1, 3)
         across_second(half, 1)
-    sweep_up(2)
     for half in (0, 1):
         arrived(half, 3, 1)
         arrived(half, 3, 3)
         across_second(half, 3)
     sweep_up(1)
     multiply_all(4, lambda i: (1 + 2 * lax.rem(i, 2), 1 + 2 * lax.div(i, 2)))
+    sweep_up(0)
     for half in (0, 1):
         arrived(half, 0, 2)
-    sweep_up(0)
     multiply_all(2, lambda i: (2 * (1 - i), 2 * i))
-    for half in (0, 1):
-        arrived(half, 2, 1)
-        arrived(half, 2, 3)
-        across_second(half, 2)
     sweep_down(1)
     for half in (0, 1):
         arrived(half, 1, 2)
@@ -360,7 +371,7 @@
         dst_ref=half_in,
         send_sem=half_sem.at[0],
         recv_sem=half_sem.at[1],
-        device_id=(lax.max(mirror, PEERS), tp),
+        device_id=(lax.max(facing_at, PEERS), tp),
         device_id_type=MESH,
     )
 
@@ -513,7 +524,7 @@
     ]
     return pl.pallas_call(
         kernel,
-        out_shape=jax.ShapeDtypeStruct((ROWS, width), BF16),
+        out_shape=pltpu.VMEM((ROWS, width), BF16),
         in_specs=[hbm] * 4 + [vmem] * 5 + [smem] * 2 + [vmem],
         out_specs=vmem,
         scratch_shapes=scratch,

time: 46.6 us -> 42.1 us (0.903)
  Pallas kernels: 44.7 us -> 41.3 us
  local copies, waits for them, and re-layouts: 1.67 us -> 0.71 us
    pallas_call x1, Pallas kernels: 44.7 us -> 41.3 us  [local(): pl.pallas_call(kernel, out_shape=pltpu.VMEM((ROWS, width), BF16), in_spec...]
    unnamed x1, local copies, waits for them, and re-layouts: 1.67 us -> 0.71 us
where the time goes in v3:
time: 42.1 us; the launch traced here: 42 us
  Pallas kernels  41.3 us (98%)
  local copies, waits for them, and re-layouts  0.71 us (2%)
    pallas_call x1, Pallas kernels, local(): pl.pallas_call(kernel, out_shape=pltpu.VMEM((ROWS, width), BF16), in_spec...  41.3 us

profile of v3, /device:TPU:224, one launch (start us, length us, event | category | flops | bytes accessed | tf_op | source)
XLA Modules:
  0.0 42.0 jit_solution(3003496522953011295)
XLA Ops:
  0.0 41.3 %shard_map.118 = bf16[256,512]{1,0:T(8,128)(2,1)S(1)} custom-call(bf16[256,256]{1,0:T(8,128)(2,1)} %tok.1, bf16[4096,512]{1,0:T(8,128)(2,1)} %wz.1, bf16[4096,512]{1,0:T(8,128)(2,1)} %wx.1, bf16[4096,128]{1,0:T(8,128)(2,1)} %wbc.1, f32[4,512]{1,0:T(4,128)} %conv_x.1, f32[4,128]{1,0:T(4,128)} %conv_bc.1, f32[1,512]{1,0:T(1,128)} %bitcast.5, ...), custom_call_target="tpu_custom_call" | custom-call | tf_op jit(solution)/shard_map/pallas_call | solution.py:525
  41.3 0.7 %copy.14 = bf16[256,512]{1,0:T(8,128)(2,1)} copy(bf16[256,512]{1,0:T(8,128)(2,1)S(1)} %shard_map.118) | data formatting | bytes 524288

commit v4 on v3

--- a/solution.py
+++ b/solution.py
@@ -13,7 +13,6 @@
 FEAT = 256
 SECTIONS = 16
 PEERS = 8
-SLICE = 64
 LT = 4
 F32 = jnp.float32
 BF16 = jnp.bfloat16
@@ -30,7 +29,7 @@
 def kernel(
     tok, wz, wx, wbc, conv_x, conv_bc, bias_x, bias_bc, decay_t, step, skip, gain, out,
     held, vz, vx, vbc, acc_z, acc_x, acc_bc, pre, rim_out, rim_in, xs, bc, seg, grow, end_w,
-    tot_out, tot_in, st_out, st_in, en_out, en_in, half_out, half_in, y, sq_out, sq_in,
+    tot_out, tot_in, st_out, st_in, en_out, en_in, half_out, half_in, within, remains, y, sq_out, sq_in,
     w_sem, own_sem, g_send, g_recv, tot_send, tot_recv, rim_sem, bc_sem, st_send, st_recv,
     en_send, en_recv, half_sem, sq_sem, up, down, facing,
 ):
@@ -48,11 +47,8 @@
     far_place = lax.rem(place + 2, 4)
     facing_at = ((1 - group) * 4 + far_place) * 2 + core
 
-    def owner(o):
-        p = lax.rem(lax.div(o, 2) + 2 * group, 4)
-        return p * 2 + lax.rem(o, 2)
-
-    mine = owner(me)
+    mine = lax.rem(place + 2 * group, 4)
+    owns = core == 1
 
     def signal(sem, section, column=None):
         pl.semaphore_signal(
@@ -131,7 +127,7 @@
         s = slot(dx, dy)
         a = held[s]
         depth = pl.ds(pl.multiple_of(s * FEAT, FEAT), FEAT)
-        for acc, v in ((acc_x, vx), (acc_bc, vbc), (acc_z, vz)):
+        for acc, v in ((acc_x, vx), (acc_bc, vbc)):
             part = dot(a, v[depth, :])
             acc[...] = part if begin else acc[...] + part
 
@@ -217,8 +213,8 @@
         arrived(half, 2, 3)
         across_second(half, 2)
     own.wait()
-    for w in weights:
-        w.wait()
+    weights[0].wait()
+    weights[1].wait()
     multiply(0, 0, True)
 
     def beside(i):
@@ -257,11 +253,12 @@
     multiply(2, 2)
     sweep_down(3)
 
+    def before_conv(t, rows):
+        p = acc_bc[rows] if t == LT else acc_x[rows, t * 128 : (t + 1) * 128]
+        return p.astype(BF16)
+
     for t in range(LT + 1):
-        p = acc_bc[...] if t == LT else acc_x[:, t * 128 : (t + 1) * 128]
-        p = p.astype(BF16)
-        rim_out[t] = p[ROWS - 16 :]
-        pre[t, 8 : 8 + ROWS] = p.astype(F32)
+        rim_out[t] = before_conv(t, slice(ROWS - 16, ROWS))
     rim = pltpu.make_async_remote_copy(
         src_ref=rim_out,
         dst_ref=rim_in,
@@ -279,21 +276,41 @@
     def _():
         rim.start()
 
-    tot_in[me] = tot_out[lax.div(mine, 2)]
-
-    def send_total(i, c):
-        q = lax.rem(me + i, PEERS)
+    for t in range(LT + 1):
+        pre[t, 8 : 8 + ROWS] = before_conv(t, slice(0, ROWS)).astype(F32)
+    def to_owners(send_one):
+        def body(i, c):
+            p = lax.rem(place + i, 4)
+            send_one(lax.rem(p + 2 * group, 4), group * PEERS + 2 * p + 1)
+            return c
+
+        lax.fori_loop(1, 4, body, 0)
+
+        @pl.when(core == 0)
+        def _():
+            send_one(mine, ctx + 1)
+
+    def send_total(piece_of, section):
         pltpu.make_async_remote_copy(
-            src_ref=tot_out.at[lax.div(owner(q), 2)],
+            src_ref=tot_out.at[piece_of],
             dst_ref=tot_in.at[me],
             send_sem=tot_send,
             recv_sem=tot_recv,
-            device_id=(group * PEERS + q, tp),
+            device_id=(section, tp),
             device_id_type=MESH,
         ).start()
-        return c
-
-    lax.fori_loop(1, PEERS, send_total, 0)
+
+    def send_state(piece_of, section):
+        pltpu.make_async_remote_copy(
+            src_ref=st_out.at[piece_of],
+            dst_ref=st_in.at[me],
+            send_sem=st_send,
+            recv_sem=st_recv.at[me],
+            device_id=(section, tp),
+            device_id_type=MESH,
+        ).start()
+
+    to_owners(send_total)
 
     @pl.when(ctx == 0)
     def _():
@@ -331,22 +348,8 @@
     b_t = bc[0].astype(F32).T.astype(BF16)
     for t in range(LT):
         weighted = (xs[t].astype(F32) * end_w[t]).astype(BF16)
-        st_out[2 * t : 2 * t + 2] = dot(b_t, weighted).reshape(2, SLICE, 128).astype(BF16)
-    st_in[me] = st_out[mine]
-
-    def send_state(i, c):
-        q = lax.rem(me + i, PEERS)
-        pltpu.make_async_remote_copy(
-            src_ref=st_out.at[owner(q)],
-            dst_ref=st_in.at[me],
-            send_sem=st_send,
-            recv_sem=st_recv.at[me],
-            device_id=(group * PEERS + q, tp),
-            device_id_type=MESH,
-        ).start()
-        return c
-
-    lax.fori_loop(1, PEERS, send_state, 0)
+        st_out[t] = dot(b_t, weighted).astype(BF16)
+    to_owners(send_state)
 
     scores = dot(bc[1], b_t)
 
@@ -357,15 +360,11 @@
 
     for t in range(LT):
         intra(t)
-    for t in range(LT):
-        g = acc_z[:, t * 128 : (t + 1) * 128].astype(BF16).astype(F32)
-        acc_z[:, t * 128 : (t + 1) * 128] = silu(g)
-
-    def all_but_one(ref, sem):
-        part = ref.at[pl.ds(0, ref.shape[0] - 1)]
+
+    def landed(ref, count, sem):
+        part = ref.at[pl.ds(0, count)]
         pltpu.make_async_copy(part, part, sem).wait()
 
-    all_but_one(tot_in, tot_recv)
     total_of_half = pltpu.make_async_remote_copy(
         src_ref=half_out,
         dst_ref=half_in,
@@ -374,14 +373,6 @@
         device_id=(lax.max(facing_at, PEERS), tp),
         device_id_type=MESH,
     )
-
-    @pl.when(group == 0)
-    def _():
-        half_in[...] = jnp.zeros_like(half_in)
-
-    @pl.when(group == 1)
-    def _():
-        total_of_half.wait_recv()
 
     def entering_copy(q):
         return pltpu.make_async_remote_copy(
@@ -396,39 +387,96 @@
     def sends(q):
         return jnp.logical_and(me != q, group * PEERS + q > 0)
 
-    state = half_in[...].astype(F32)
-    for q in range(PEERS):
-        en_out[q] = state.astype(BF16)
-
+    def state_of(q):
+        @pl.when(me != q)
+        def _():
+            pltpu.make_async_copy(st_in.at[q], st_in.at[q], st_recv.at[q]).wait()
+
+        return st_in[q].astype(F32)
+
+    def send_entering(q):
         @pl.when(sends(q))
-        def _(q=q):
+        def _():
             entering_copy(q).start()
 
-        @pl.when(me != q)
-        def _(q=q):
-            pltpu.make_async_copy(st_in.at[q], st_in.at[q], st_recv.at[q]).wait()
-
-        state = tot_in[q][0:1] * state + st_in[q].astype(F32)
-    half_out[...] = state.astype(BF16)
-
     @pl.when(group == 0)
     def _():
         pl.semaphore_wait(facing, 1)
+
+    @pl.when(owns)
+    def _():
+        tot_in[me] = tot_out[mine]
+        st_in[me] = st_out[mine]
+        landed(tot_in, PEERS - 1, tot_recv)
+
+    @pl.when(jnp.logical_and(owns, group == 0))
+    def _():
+        state = jnp.zeros((128, 128), F32)
+        for q in range(PEERS):
+            en_out[q] = state.astype(BF16)
+            send_entering(q)
+            state = tot_in[q][0:1] * state + state_of(q)
+        half_out[...] = state.astype(BF16)
+
+    @pl.when(jnp.logical_and(owns, group == 1))
+    def _():
+        state = jnp.zeros((128, 128), F32)
+        left = jnp.ones((8, 128), F32)
+        for q in range(PEERS):
+            within[q] = state
+            remains[q] = left
+            state = tot_in[q][0:1] * state + state_of(q)
+            left = tot_in[q] * left
+        total_of_half.wait_recv()
+        half = half_in[...].astype(F32)
+
+        def body(i, c):
+            q = jnp.where(place < 2, PEERS - 1 - i, i)
+            en_out[q] = (within[q] + remains[q][0:1] * half).astype(BF16)
+            send_entering(q)
+            return c
+
+        lax.fori_loop(0, PEERS, body, 0)
+
+    @pl.when(owns)
+    def _():
+        en_in[mine] = en_out[me]
+
+    @pl.when(jnp.logical_and(owns, group == 0))
+    def _():
         total_of_half.start()
 
-    en_in[mine] = en_out[me]
+    weights[2].wait()
+    acc_z[...] = jnp.zeros_like(acc_z)
+
+    def gate(i, c):
+        total = acc_z[...]
+        for k in range(4):
+            depth = pl.ds(pl.multiple_of((4 * i + k) * FEAT, FEAT), FEAT)
+            total = total + dot(held[4 * i + k], vz[depth, :])
+        acc_z[...] = total
+        return c
+
+    lax.fori_loop(0, 4, gate, 0)
+    for t in range(LT):
+        g = acc_z[:, t * 128 : (t + 1) * 128].astype(BF16).astype(F32)
+        acc_z[:, t * 128 : (t + 1) * 128] = silu(g)
 
     @pl.when(ctx == 0)
     def _():
         en_in[...] = jnp.zeros_like(en_in)
 
-    @pl.when(ctx > 0)
-    def _():
-        all_but_one(en_in, en_recv)
+    @pl.when(owns)
+    def _():
+        landed(en_in, 3, en_recv)
+
+    @pl.when(jnp.logical_and(ctx > 0, core == 0))
+    def _():
+        landed(en_in, 4, en_recv)
 
     squares = jnp.zeros((ROWS, 128), F32)
     for t in range(LT):
-        entering = en_in[2 * t : 2 * t + 2].reshape(128, 128)
+        entering = en_in[t]
         gated = (y[t] + grow[t] * dot(bc[1], entering)) * acc_z[:, t * 128 : (t + 1) * 128]
         squares = squares + gated * gated
         y[t] = gated
@@ -452,21 +500,29 @@
 
     norm.wait_send()
     swap.wait_send()
-    all_but_one(held, g_send)
-    all_but_one(tot_in, tot_send)
-    all_but_one(st_out, st_send)
+    landed(held, 15, g_send)
+
+    @pl.when(owns)
+    def _():
+        landed(tot_out, 3, tot_send)
+        landed(st_out, 3, st_send)
+
+    @pl.when(core == 0)
+    def _():
+        landed(tot_out, 4, tot_send)
+        landed(st_out, 4, st_send)
 
     @pl.when(ctx < SECTIONS - 1)
     def _():
         rim.wait_send()
 
-    @pl.when(group == 0)
+    @pl.when(jnp.logical_and(owns, group == 0))
     def _():
         total_of_half.wait_send()
 
     for q in range(PEERS):
 
-        @pl.when(sends(q))
+        @pl.when(jnp.logical_and(owns, sends(q)))
         def _(q=q):
             entering_copy(q).wait_send()
 
@@ -495,12 +551,14 @@
         pltpu.VMEM((LT, ROWS, 128), F32),
         pltpu.VMEM((LT, 8, 128), F32),
         pltpu.VMEM((PEERS, 8, 128), F32),
-        pltpu.VMEM((PEERS, SLICE, 128), BF16),
-        pltpu.VMEM((PEERS, SLICE, 128), BF16),
-        pltpu.VMEM((PEERS, SLICE, 128), BF16),
-        pltpu.VMEM((PEERS, SLICE, 128), BF16),
-        pltpu.VMEM((SLICE, 128), BF16),
-        pltpu.VMEM((SLICE, 128), BF16),
+        pltpu.VMEM((LT, 128, 128), BF16),
+        pltpu.VMEM((PEERS, 128, 128), BF16),
+        pltpu.VMEM((PEERS, 128, 128), BF16),
+        pltpu.VMEM((LT, 128, 128), BF16),
+        pltpu.VMEM((128, 128), BF16),
+        pltpu.VMEM((128, 128), BF16),
+        pltpu.VMEM((PEERS, 128, 128), F32),
+        pltpu.VMEM((PEERS, 8, 128), F32),
         pltpu.VMEM((LT, ROWS, 128), F32),
         pltpu.VMEM((8, ROWS), F32),
         pltpu.VMEM((8, ROWS), F32),

time: 42.1 us -> 41.4 us (0.983); the launches traced: 42 us -> 40.7 us
  Pallas kernels: 41.3 us -> 40 us
    pallas_call x1, Pallas kernels: 41.3 us -> 40 us  [local(): pl.pallas_call(kernel, out_shape=pltpu.VMEM((ROWS, width), BF16), in_spec...]
where the time goes in v4:
time: 41.4 us; the launch traced here: 40.7 us
  Pallas kernels  40 us (97%)
  local copies, waits for them, and re-layouts  0.71 us (2%)
    pallas_call x1, Pallas kernels, local(): pl.pallas_call(kernel, out_shape=pltpu.VMEM((ROWS, width), BF16), in_spec...  40 us

profile of v4, /device:TPU:224, one launch (start us, length us, event | category | flops | bytes accessed | tf_op | source)
XLA Modules:
  0.0 40.7 jit_solution(11953909599942760457)
XLA Ops:
  0.0 40.0 %shard_map.118 = bf16[256,512]{1,0:T(8,128)(2,1)S(1)} custom-call(bf16[256,256]{1,0:T(8,128)(2,1)} %tok.1, bf16[4096,512]{1,0:T(8,128)(2,1)} %wz.1, bf16[4096,512]{1,0:T(8,128)(2,1)} %wx.1, bf16[4096,128]{1,0:T(8,128)(2,1)} %wbc.1, f32[4,512]{1,0:T(4,128)} %conv_x.1, f32[4,128]{1,0:T(4,128)} %conv_bc.1, f32[1,512]{1,0:T(1,128)} %bitcast.5, ...), custom_call_target="tpu_custom_call" | custom-call | tf_op jit(solution)/shard_map/pallas_call | solution.py:583
  40.0 0.7 %copy.14 = bf16[256,512]{1,0:T(8,128)(2,1)} copy(bf16[256,512]{1,0:T(8,128)(2,1)S(1)} %shard_map.118) | data formatting | bytes 524288

commit v5 on v4

--- a/solution.py
+++ b/solution.py
@@ -310,40 +310,51 @@
             device_id_type=MESH,
         ).start()
 
-    to_owners(send_total)
-
-    @pl.when(ctx == 0)
-    def _():
-        rim_in[...] = jnp.zeros_like(rim_in)
-
-    @pl.when(ctx > 0)
-    def _():
-        rim.wait_recv()
-
-    def conv(t):
-        pre[t, 0:8] = rim_in[t].astype(F32)[8:]
+    def conv(t, low, high):
         cols = slice(0, 128) if t == LT else slice(t * 128, (t + 1) * 128)
         taps, bias = (conv_bc, bias_bc) if t == LT else (conv_x, bias_x)
-        total = bias[:, cols] + jnp.zeros((ROWS, 128), F32)
+        total = bias[:, cols] + jnp.zeros((high - low, 128), F32)
         for k in range(TAPS):
-            total = total + taps[k : k + 1, cols] * pre[t, 5 + k : 5 + k + ROWS]
+            total = total + taps[k : k + 1, cols] * pre[t, 5 + k + low : 5 + k + high]
         return silu(total).astype(BF16)
 
     side = lax.rem(tp, 2)
-    bc[side] = conv(LT)
-    swap = pltpu.make_async_remote_copy(
-        src_ref=bc.at[side],
-        dst_ref=bc.at[side],
-        send_sem=bc_sem.at[0],
-        recv_sem=bc_sem.at[1],
-        device_id=(ctx, mate),
-        device_id_type=MESH,
-    )
-    swap.start()
-    for t in range(LT):
-        xs[t] = conv(t)
-    other = bc.at[1 - side]
-    pltpu.make_async_copy(other, other, bc_sem.at[1]).wait()
+
+    def swap(which, low, high):
+        part = bc.at[side, pl.ds(low, high - low)]
+        return pltpu.make_async_remote_copy(
+            src_ref=part,
+            dst_ref=part,
+            send_sem=bc_sem.at[0, which],
+            recv_sem=bc_sem.at[1, which],
+            device_id=(ctx, mate),
+            device_id_type=MESH,
+        )
+
+    most, first_rows = swap(0, 16, ROWS), swap(1, 0, 16)
+    bc[side, 16:ROWS] = conv(LT, 16, ROWS)
+    most.start()
+    for t in range(LT):
+        xs[t, 16:ROWS] = conv(t, 16, ROWS)
+    to_owners(send_total)
+
+    @pl.when(ctx == 0)
+    def _():
+        rim_in[...] = jnp.zeros_like(rim_in)
+
+    @pl.when(ctx > 0)
+    def _():
+        rim.wait_recv()
+
+    for t in range(LT + 1):
+        pre[t, 0:8] = rim_in[t].astype(F32)[8:]
+    bc[side, 0:16] = conv(LT, 0, 16)
+    first_rows.start()
+    for t in range(LT):
+        xs[t, 0:16] = conv(t, 0, 16)
+    for which, low, high in ((0, 16, ROWS), (1, 0, 16)):
+        other = bc.at[1 - side, pl.ds(low, high - low)]
+        pltpu.make_async_copy(other, other, bc_sem.at[1, which]).wait()
 
     b_t = bc[0].astype(F32).T.astype(BF16)
     for t in range(LT):
@@ -431,7 +442,7 @@
         half = half_in[...].astype(F32)
 
         def body(i, c):
-            q = jnp.where(place < 2, PEERS - 1 - i, i)
+            q = jnp.where(place < 2, 2 * (3 - lax.div(i, 2)) + lax.rem(i, 2), i)
             en_out[q] = (within[q] + remains[q][0:1] * half).astype(BF16)
             send_entering(q)
             return c
@@ -499,7 +510,8 @@
         out[:, cols] = (y[t] * scale * gain[:, cols]).astype(BF16)
 
     norm.wait_send()
-    swap.wait_send()
+    most.wait_send()
+    first_rows.wait_send()
     landed(held, 15, g_send)
 
     @pl.when(owns)
@@ -569,7 +581,7 @@
         dma,
         dma,
         dma((2,)),
-        dma((2,)),
+        dma((2, 2)),
         dma,
         dma((PEERS,)),
         dma((PEERS,)),

time: 41.4 us -> 40 us (0.966)
  Pallas kernels: 40 us -> 38.7 us
    pallas_call x1, Pallas kernels: 40 us -> 38.7 us  [local(): pl.pallas_call(kernel, out_shape=pltpu.VMEM((ROWS, width), BF16), in_spec...]
where the time goes in v5:
time: 40 us; the launch traced here: 39.4 us
  Pallas kernels  38.7 us (97%)
  local copies, waits for them, and re-layouts  0.71 us (2%)
    pallas_call x1, Pallas kernels, local(): pl.pallas_call(kernel, out_shape=pltpu.VMEM((ROWS, width), BF16), in_spec...  38.7 us

profile of v5, /device:TPU:224, one launch (start us, length us, event | category | flops | bytes accessed | tf_op | source)
XLA Modules:
  0.0 39.4 jit_solution(18046503683948541148)
XLA Ops:
  0.0 38.7 %shard_map.118 = bf16[256,512]{1,0:T(8,128)(2,1)S(1)} custom-call(bf16[256,256]{1,0:T(8,128)(2,1)} %tok.1, bf16[4096,512]{1,0:T(8,128)(2,1)} %wz.1, bf16[4096,512]{1,0:T(8,128)(2,1)} %wx.1, bf16[4096,128]{1,0:T(8,128)(2,1)} %wbc.1, f32[4,512]{1,0:T(4,128)} %conv_x.1, f32[4,128]{1,0:T(4,128)} %conv_bc.1, f32[1,512]{1,0:T(1,128)} %bitcast.5, ...), custom_call_target="tpu_custom_call" | custom-call | tf_op jit(solution)/shard_map/pallas_call | solution.py:595
  38.7 0.7 %copy.14 = bf16[256,512]{1,0:T(8,128)(2,1)} copy(bf16[256,512]{1,0:T(8,128)(2,1)S(1)} %shard_map.118) | data formatting | bytes 524288

commit v6 on v5

--- a/solution.py
+++ b/solution.py
@@ -29,9 +29,9 @@
 def kernel(
     tok, wz, wx, wbc, conv_x, conv_bc, bias_x, bias_bc, decay_t, step, skip, gain, out,
     held, vz, vx, vbc, acc_z, acc_x, acc_bc, pre, rim_out, rim_in, xs, bc, seg, grow, end_w,
-    tot_out, tot_in, st_out, st_in, en_out, en_in, half_out, half_in, within, remains, y, sq_out, sq_in,
+    tot_out, tot_in, st_out, st_in, en_out, en_in, half_out, half_in, within, remains, mate_st, mate_tot, y, sq_out, sq_in,
     w_sem, own_sem, g_send, g_recv, tot_send, tot_recv, rim_sem, bc_sem, st_send, st_recv,
-    en_send, en_recv, half_sem, sq_sem, up, down, facing,
+    en_send, en_recv, half_sem, sq_sem, pair_sem, up, down, facing,
 ):
     ctx, tp = lax.axis_index("ctx"), lax.axis_index("tp")
     core = lax.rem(ctx, 2)
@@ -362,6 +362,26 @@
         st_out[t] = dot(b_t, weighted).astype(BF16)
     to_owners(send_state)
 
+    def to_pair(src, dst, which):
+        return pltpu.make_async_remote_copy(
+            src_ref=src,
+            dst_ref=dst,
+            send_sem=pair_sem.at[0, which],
+            recv_sem=pair_sem.at[1, which],
+            device_id=(ctx + 1 - 2 * core, tp),
+            device_id_type=MESH,
+        )
+
+    pair_state = to_pair(st_out, mate_st, 0)
+    pair_total = to_pair(tot_out, mate_tot, 1)
+    pair_entering = to_pair(en_in, en_in, 2)
+
+    @pl.when(core == 0)
+    def _():
+        pair_state.start()
+        pair_total.start()
+
+
     scores = dot(bc[1], b_t)
 
     def intra(t):
@@ -396,7 +416,7 @@
         )
 
     def sends(q):
-        return jnp.logical_and(me != q, group * PEERS + q > 0)
+        return jnp.logical_and(lax.rem(q, 2) == 0, group * PEERS + q > 0)
 
     def state_of(q):
         @pl.when(me != q)
@@ -442,16 +462,12 @@
         half = half_in[...].astype(F32)
 
         def body(i, c):
-            q = jnp.where(place < 2, 2 * (3 - lax.div(i, 2)) + lax.rem(i, 2), i)
+            q = 2 * jnp.where(place < 2, 3 - i, i)
             en_out[q] = (within[q] + remains[q][0:1] * half).astype(BF16)
             send_entering(q)
             return c
 
-        lax.fori_loop(0, PEERS, body, 0)
-
-    @pl.when(owns)
-    def _():
-        en_in[mine] = en_out[me]
+        lax.fori_loop(0, PEERS // 2, body, 0)
 
     @pl.when(jnp.logical_and(owns, group == 0))
     def _():
@@ -477,13 +493,22 @@
     def _():
         en_in[...] = jnp.zeros_like(en_in)
 
+    @pl.when(jnp.logical_and(ctx > 0, core == 0))
+    def _():
+        landed(en_in, 4, en_recv)
+
+    @pl.when(core == 0)
+    def _():
+        pair_entering.start()
+
     @pl.when(owns)
     def _():
-        landed(en_in, 3, en_recv)
-
-    @pl.when(jnp.logical_and(ctx > 0, core == 0))
-    def _():
-        landed(en_in, 4, en_recv)
+        pair_state.wait_recv()
+        pair_total.wait_recv()
+        pair_entering.wait_recv()
+        for t in range(LT):
+            passed = mate_tot[t][0:1] * en_in[t].astype(F32) + mate_st[t].astype(F32)
+            en_in[t] = passed.astype(BF16)
 
     squares = jnp.zeros((ROWS, 128), F32)
     for t in range(LT):
@@ -523,6 +548,9 @@
     def _():
         landed(tot_out, 4, tot_send)
         landed(st_out, 4, st_send)
+        pair_state.wait_send()
+        pair_total.wait_send()
+        pair_entering.wait_send()
 
     @pl.when(ctx < SECTIONS - 1)
     def _():
@@ -571,6 +599,8 @@
         pltpu.VMEM((128, 128), BF16),
         pltpu.VMEM((PEERS, 128, 128), F32),
         pltpu.VMEM((PEERS, 8, 128), F32),
+        pltpu.VMEM((LT, 128, 128), BF16),
+        pltpu.VMEM((LT, 8, 128), F32),
         pltpu.VMEM((LT, ROWS, 128), F32),
         pltpu.VMEM((8, ROWS), F32),
         pltpu.VMEM((8, ROWS), F32),
@@ -588,6 +618,7 @@
         dma,
         dma((2,)),
         dma((2,)),
+        dma((2, 3)),
         pltpu.SemaphoreType.REGULAR,
         pltpu.SemaphoreType.REGULAR,
         pltpu.SemaphoreType.REGULAR,

time: 40 us -> 39.2 us (0.980)
  the two profiles are of different devices: /device:TPU:224 before, /device:TPU:161 now
where the time goes in v6:
time: 39.2 us; the launch traced here: 39.1 us
  Pallas kernels  38.3 us (98%)
  local copies, waits for them, and re-layouts  0.71 us (2%)
    pallas_call x1, Pallas kernels, local(): pl.pallas_call(kernel, out_shape=pltpu.VMEM((ROWS, width), BF16), in_spec...  38.3 us

profile of v6, /device:TPU:161, one launch (start us, length us, event | category | flops | bytes accessed | tf_op | source)
XLA Modules:
  0.0 39.1 jit_solution(4404558067321311920)
XLA Ops:
  0.0 38.3 %shard_map.118 = bf16[256,512]{1,0:T(8,128)(2,1)S(1)} custom-call(bf16[256,256]{1,0:T(8,128)(2,1)} %tok.1, bf16[4096,512]{1,0:T(8,128)(2,1)} %wz.1, bf16[4096,512]{1,0:T(8,128)(2,1)} %wx.1, bf16[4096,128]{1,0:T(8,128)(2,1)} %wbc.1, f32[4,512]{1,0:T(4,128)} %conv_x.1, f32[4,128]{1,0:T(4,128)} %conv_bc.1, f32[1,512]{1,0:T(1,128)} %bitcast.5, ...), custom_call_target="tpu_custom_call" | custom-call | tf_op jit(solution)/shard_map/pallas_call | solution.py:626
  38.4 0.7 %copy.14 = bf16[256,512]{1,0:T(8,128)(2,1)} copy(bf16[256,512]{1,0:T(8,128)(2,1)S(1)} %shard_map.118) | data formatting | bytes 524288

commit v7 on v6

--- a/solution.py
+++ b/solution.py
@@ -107,21 +107,13 @@
         pltpu.make_async_copy(p, p, g_recv.at[half, first * SIDE + second]).wait()
 
     def along_second(half, first):
-        if first == 3:
-
-            @pl.when(core == 0)
-            def _():
-                send(half, (first, 0), 2, 1, (first, 2))
-
         send(half, (first, 0), 1, 1, (first, 1))
         send(half, (first, 0), -1, 1, (first, 3))
 
     def across_second(half, first):
         flag = lax.rem(first + core, 2)
 
-        @pl.when(jnp.logical_or(core == 1, first < 3))
-        def _():
-            send(half, (first, 1 + 2 * flag), 1 - 2 * flag, 1, (first, 2))
+        send(half, (first, 1 + 2 * flag), 1 - 2 * flag, 1, (first, 2))
 
     def multiply(dx, dy, begin=False):
         s = slot(dx, dy)

time: 39.2 us -> 38.8 us (0.990)
  no operation moved by 1% of the time
where the time goes in v7:
time: 38.8 us; the launch traced here: 38.7 us
  Pallas kernels  38 us (98%)
  local copies, waits for them, and re-layouts  0.71 us (2%)
    pallas_call x1, Pallas kernels, local(): pl.pallas_call(kernel, out_shape=pltpu.VMEM((ROWS, width), BF16), in_spec...  38 us

profile of v7, /device:TPU:161, one launch (start us, length us, event | category | flops | bytes accessed | tf_op | source)
XLA Modules:
  0.0 38.7 jit_solution(7865451850218063230)
XLA Ops:
  0.0 38.0 %shard_map.118 = bf16[256,512]{1,0:T(8,128)(2,1)S(1)} custom-call(bf16[256,256]{1,0:T(8,128)(2,1)} %tok.1, bf16[4096,512]{1,0:T(8,128)(2,1)} %wz.1, bf16[4096,512]{1,0:T(8,128)(2,1)} %wx.1, bf16[4096,128]{1,0:T(8,128)(2,1)} %wbc.1, f32[4,512]{1,0:T(4,128)} %conv_x.1, f32[4,128]{1,0:T(4,128)} %conv_bc.1, f32[1,512]{1,0:T(1,128)} %bitcast.5, ...), custom_call_target="tpu_custom_call" | custom-call | tf_op jit(solution)/shard_map/pallas_call | solution.py:618
  38.0 0.7 %copy.14 = bf16[256,512]{1,0:T(8,128)(2,1)} copy(bf16[256,512]{1,0:T(8,128)(2,1)S(1)} %shard_map.118) | data formatting | bytes 524288
